TPU v7x, 32 devices: a whole 2x2x4 slice. The times are simulated.
32 devices in a mesh: gx: 8 (over y, x, core), gy: 4 (over z).
Axes of the slice: x: 2, y: 2, z: 4, core: 2. Of those that a mesh axis runs over, the one named last changes fastest.
Arguments:
- momenta: float32 [3, 16, 32, 1024], P(None, None, 'gy', 'gx'), may hold values from -6 to 6
- theta: float32 [16, 32, 1024], P(None, 'gy', 'gx'), may hold values from -6 to 6
- courant: float32 [3, 16, 32, 1024], P(None, None, 'gy', 'gx'), may hold values from -0.3 to 0.3
- density: float32 [16, 32, 1024], P(None, 'gy', 'gx'), may hold values from 0.8 to 1.6
- metric_diag: float32 [3, 16, 32, 1024], P(None, None, 'gy', 'gx'), may hold values from 0.5 to 2
- metric_cross: float32 [3, 16, 32, 1024], P(None, None, 'gy', 'gx'), may hold values from -0.2 to 0.2
Outputs:
- momenta_out: float32 [3, 16, 32, 1024], P(None, None, 'gy', 'gx')
- theta_out: float32 [16, 32, 1024], P(None, 'gy', 'gx')
- pressure: float32 [16, 32, 1024], P(None, 'gy', 'gx')
All inputs are finite; a program needn't handle non-finite values.
Results may differ from a plain program's by a relative error of at most 0.0003.
Values sent between devices are 32-bit elements; how exact they have to be, the bound alone decides.
A program may use at most 64 MiB of HBM per device.

v0:
```python
import jax
import jax.numpy as jnp
from jax import lax
from jax.sharding import PartitionSpec as P

ITERS = 3


helm = 0.02


def extended(cells, sides, width):
    for axis, dim in sides:
        count = lax.axis_size(axis)
        head = lax.slice_in_dim(cells, 0, width, axis=dim)
        tail = lax.slice_in_dim(cells, cells.shape[dim] - width, cells.shape[dim], axis=dim)
        cells = jnp.concatenate(
            [
                lax.ppermute(tail, axis, [(i, (i + 1) % count) for i in range(count)]),
                cells,
                lax.ppermute(head, axis, [((i + 1) % count, i) for i in range(count)]),
            ],
            axis=dim,
        )
    return cells


def zshift(a, dz):
    if dz == 0:
        return a
    if dz > 0:
        return jnp.concatenate((a[..., dz:, :, :], jnp.zeros_like(a[..., :dz, :, :])), axis=-3)
    return jnp.concatenate((jnp.zeros_like(a[..., dz:, :, :]), a[..., :dz, :, :]), axis=-3)


def make_look(width, margin):

    def look(a, dz, dy, dx):
        span_y = a.shape[-2] - 2 * (width - margin)
        span_x = a.shape[-1] - 2 * (width - margin)
        start_y = width - margin + dy
        start_x = width - margin + dx
        return zshift(a[..., start_y : start_y + span_y, start_x : start_x + span_x], dz)

    return look


def donor(left, right, courant):
    return jnp.maximum(courant, 0.0) * left + jnp.minimum(courant, 0.0) * right


def antidiff(left, right, courant, dens_left, dens_right):
    return (
        0.5
        * (jnp.abs(courant) - courant * courant / (0.5 * (dens_left + dens_right)))
        * (right - left)
    )


def upwind_pass(look, field, dens, cx, cy, cz):
    centre = look(field, 0, 0, 0)
    fxr = donor(centre, look(field, 0, 0, 1), look(cx, 0, 0, 1))
    fxl = donor(look(field, 0, 0, -1), centre, look(cx, 0, 0, 0))
    fyr = donor(centre, look(field, 0, 1, 0), look(cy, 0, 1, 0))
    fyl = donor(look(field, 0, -1, 0), centre, look(cy, 0, 0, 0))
    fzr = donor(centre, look(field, 1, 0, 0), look(cz, 1, 0, 0))
    fzl = donor(look(field, -1, 0, 0), centre, look(cz, 0, 0, 0))
    return centre - (fxr - fxl + fyr - fyl + fzr - fzl) / look(dens, 0, 0, 0)


def anti_pass(look_new, look_old, first, dens, cx, cy, cz):
    centre = look_new(first, 0, 0, 0)
    here = look_old(dens, 0, 0, 0)
    axr = antidiff(
        centre, look_new(first, 0, 0, 1), look_old(cx, 0, 0, 1), here, look_old(dens, 0, 0, 1)
    )
    axl = antidiff(
        look_new(first, 0, 0, -1), centre, look_old(cx, 0, 0, 0), look_old(dens, 0, 0, -1), here
    )
    ayr = antidiff(
        centre, look_new(first, 0, 1, 0), look_old(cy, 0, 1, 0), here, look_old(dens, 0, 1, 0)
    )
    ayl = antidiff(
        look_new(first, 0, -1, 0), centre, look_old(cy, 0, 0, 0), look_old(dens, 0, -1, 0), here
    )
    azr = antidiff(
        centre, look_new(first, 1, 0, 0), look_old(cz, 1, 0, 0), here, look_old(dens, 1, 0, 0)
    )
    azl = antidiff(
        look_new(first, -1, 0, 0), centre, look_old(cz, 0, 0, 0), look_old(dens, -1, 0, 0), here
    )
    return centre - (axr - axl + ayr - ayl + azr - azl) / here


def coefficients(look, a_one, a_two, a_three, cross, upper_y, lower_y, upper_z, lower_z):
    wx = 0.5 * (look(a_one, 0, 0, 0) + look(a_one, 0, 0, 1))
    wxl = 0.5 * (look(a_one, 0, 0, -1) + look(a_one, 0, 0, 0))
    wy = 0.5 * (look(a_two, 0, 0, 0) + look(a_two, 0, 1, 0)) * upper_y
    wyl = 0.5 * (look(a_two, 0, -1, 0) + look(a_two, 0, 0, 0)) * lower_y
    wz = 0.5 * (a_three + zshift(a_three, 1)) * upper_z
    wzl = 0.5 * (zshift(a_three, -1) + a_three) * lower_z
    return (wx, wxl, wy, wyl, wz, wzl, cross[0], cross[1], cross[2])


def operate(look, field, coef):
    wx, wxl, wy, wyl, wz, wzl, c_xy, c_xz, c_yz = coef
    centre = look(field, 0, 0, 0)
    flow_x = wx * (look(field, 0, 0, 1) - centre) - wxl * (centre - look(field, 0, 0, -1))
    flow_y = wy * (look(field, 0, 1, 0) - centre) - wyl * (centre - look(field, 0, -1, 0))
    flow_z = wz * (look(field, 1, 0, 0) - centre) - wzl * (centre - look(field, -1, 0, 0))
    d_xy = 0.25 * (
        look(field, 0, 1, 1)
        - look(field, 0, 1, -1)
        - (look(field, 0, -1, 1) - look(field, 0, -1, -1))
    )
    d_xz = 0.25 * (
        look(field, 1, 0, 1)
        - look(field, 1, 0, -1)
        - (look(field, -1, 0, 1) - look(field, -1, 0, -1))
    )
    d_yz = 0.25 * (
        look(field, 1, 1, 0)
        - look(field, 1, -1, 0)
        - (look(field, -1, 1, 0) - look(field, -1, -1, 0))
    )
    return flow_x + flow_y + flow_z + c_xy * d_xy + c_xz * d_xz + c_yz * d_yz - helm * centre


def local(momenta, theta, courant, density, metric_diag, metric_cross):
    levels_count = density.shape[0]
    rows_dev = density.shape[1]
    total_rows = rows_dev * lax.axis_size("gy")
    first_row = lax.axis_index("gy") * rows_dev
    levels = jnp.arange(levels_count, dtype=jnp.int32)[:, None, None]
    level_mask = (levels != 0).astype(jnp.float32)
    packed = jnp.concatenate((momenta, theta[None], density[None], courant), axis=0)
    global_rows = first_row + jnp.arange(rows_dev + 2 * 1, dtype=jnp.int32) - 1
    inside = ((global_rows >= 0) & (global_rows < total_rows))[:, None]
    not_first = (global_rows != 0).astype(jnp.float32)[:, None]
    look_one = make_look(1, 0)
    narrow = extended(packed, (("gx", 3), ("gy", 2)), 1)
    narrow = jnp.where(inside, narrow, 0.0)
    dens_pad = narrow[4]
    cy_pad = narrow[6] * not_first
    cz_pad = narrow[7] * level_mask
    first = upwind_pass(look_one, narrow[0:4], dens_pad, narrow[5], cy_pad, cz_pad)
    first_pad = extended(first, (("gx", 3), ("gy", 2)), 1)
    first_pad = jnp.where(inside, first_pad, 0.0)
    moved = anti_pass(look_one, look_one, first_pad, dens_pad, narrow[5], cy_pad, cz_pad)
    flows = jnp.concatenate((moved[0:2], metric_diag[0:2]), axis=0)
    flows_pad = extended(flows, (("gx", 3), ("gy", 2)), 1)
    flows_pad = jnp.where(inside, flows_pad, 0.0)
    rhs = (
        0.5 * (look_one(flows_pad[0], 0, 0, 1) - look_one(flows_pad[0], 0, 0, -1))
        + 0.5 * (look_one(flows_pad[1], 0, 1, 0) - look_one(flows_pad[1], 0, -1, 0))
        + 0.5 * (zshift(moved[2], 1) - zshift(moved[2], -1))
    )
    global_rows = (first_row + jnp.arange(rows_dev, dtype=jnp.int32))[:, None]
    upper_y = (global_rows < total_rows - 1).astype(jnp.float32)
    lower_y = (global_rows > 0).astype(jnp.float32)
    upper_z = (levels < levels_count - 1).astype(jnp.float32)
    lower_z = (levels > 0).astype(jnp.float32)
    coef = coefficients(
        look_one,
        flows_pad[2],
        flows_pad[3],
        metric_diag[2],
        metric_cross,
        upper_y,
        lower_y,
        upper_z,
        lower_z,
    )

    def apply_operator(field):
        padded = extended(field, (("gx", 2), ("gy", 1)), 1)
        padded = jnp.where(inside, padded, 0.0)
        return (operate(look_one, padded, coef), padded)

    solution = jnp.zeros_like(rhs)
    resid = rhs
    dirs = [resid]
    first_image, first_pad_dir = apply_operator(resid)
    images = [first_image]
    along, norm_first = lax.psum(
        (jnp.sum(resid * images[0]), jnp.sum(images[0] * images[0])), ("gx", "gy")
    )
    norms = [norm_first]
    for step in range(ITERS):
        beta = along / norms[step]
        solution = solution + beta * dirs[step]
        resid = resid - beta * images[step]
        if step + 1 < ITERS:
            lifted, resid_pad = apply_operator(resid)
            alphas = []
            locals_proj = jnp.stack([jnp.sum(lifted * image) for image in images])
            totals = lax.psum(locals_proj, ("gx", "gy"))
            new_dir = resid
            new_img = lifted
            for back in range(step + 1):
                alpha = totals[back] / norms[back]
                alphas.append(alpha)
                new_dir = new_dir - alpha * dirs[back]
                new_img = new_img - alpha * images[back]
            along, new_norm = lax.psum(
                (jnp.sum(resid * new_img), jnp.sum(new_img * new_img)), ("gx", "gy")
            )
            dirs.append(new_dir)
            images.append(new_img)
            norms.append(new_norm)
    pressure_pad = extended(solution, (("gx", 2), ("gy", 1)), 1)
    pressure_pad = jnp.where(inside, pressure_pad, 0.0)
    grad_x = 0.5 * (look_one(pressure_pad, 0, 0, 1) - look_one(pressure_pad, 0, 0, -1))
    grad_y = 0.5 * (look_one(pressure_pad, 0, 1, 0) - look_one(pressure_pad, 0, -1, 0))
    grad_z = 0.5 * (zshift(solution, 1) - zshift(solution, -1))
    momenta_out = jnp.stack((moved[0] - grad_x, moved[1] - grad_y, moved[2] - grad_z), axis=0)
    return (momenta_out, moved[3], solution)


def solution(mesh):
    placed = (
        P(None, None, "gy", "gx"),
        P(None, "gy", "gx"),
        P(None, None, "gy", "gx"),
        P(None, "gy", "gx"),
        P(None, None, "gy", "gx"),
        P(None, None, "gy", "gx"),
    )
    return jax.shard_map(
        local,
        mesh=mesh,
        in_specs=placed,
        out_specs=(P(None, None, "gy", "gx"), P(None, "gy", "gx"), P(None, "gy", "gx")),
        check_vma=False,
    )
```

profile of v0, /device:TPU:0, one launch (start us, length us, event | category | flops | bytes accessed | tf_op | source)
XLA Modules:
  0.0 326.8 jit_solution(8324345117442562653)
XLA Ops:
  0.7 1.2 pad_maximum_fusion
  1.9 0.2 fusion.109
  2.1 0.5 collective-permute-start
  2.6 2.9 collective-permute-start.1
  5.5 9.7 %collective-permute-done = f32[8,16,8,1]{3,2,1,0:T(8,128)S(1)} collective-permute-done((f32[8,16,8,1]{3,2,1,0:T(8,128)S(1)}, f32[8,16,8,1]{3,2,1,0:T(8,128)S(1)}, u32[]{:S(2)}, u32[]{:S(2)}) %collective-permute-start) | collective-permute-done | bytes 4128 | tf_op jit(solution)/shard_map/ppermute | solution.py:19
  15.3 1.5 collective-permute-done.1
  16.8 0.9 pad_maximum_fusion.8
  17.7 1.6 collective-permute-start.2
  19.3 2.2 collective-permute-start.3
  21.6 3.6 %collective-permute-done.2 = f32[8,16,1,130]{3,2,1,0:T(1,128)S(1)} collective-permute-done((f32[8,16,1,130]{3,2,1,0:T(1,128)S(1)}, f32[8,16,1,130]{3,2,1,0:T(1,128)S(1)}, u32[]{:S(2)}, u32[]{:S(2)}) %collective-permute-start.2) | collective-permute-done | bytes 66592 | tf_op jit(solution)/shard_map/ppermute | solution.py:19
  25.2 3.0 collective-permute-done.3
  28.2 1.1 maximum_select_fusion
  30.2 0.4 fusion.17
  30.7 0.2 collective-permute-start.4
  30.9 2.5 collective-permute-start.5
  33.4 5.8 %collective-permute-done.4 = f32[4,16,8,1]{3,2,1,0:T(8,128)S(1)} collective-permute-done((f32[4,16,8,1]{3,2,1,0:T(8,128)S(1)}, f32[4,16,8,1]{3,2,1,0:T(8,128)S(1)}, u32[]{:S(2)}, u32[]{:S(2)}) %collective-permute-start.4) | collective-permute-done | bytes 2080 | tf_op jit(solution)/shard_map/ppermute | solution.py:19
  39.2 0.5 pad_maximum_fusion.15
  39.7 1.1 collective-permute-start.6
  40.8 2.8 collective-permute-start.7
  43.6 3.0 collective-permute-done.6
  46.5 0.6 collective-permute-done.7
  47.1 0.6 maximum_select_fusion.1
  47.8 0.4 fusion.5
  48.4 2.6 collective-permute-start.9
  51.1 5.9 %collective-permute-done.8 = f32[4,16,8,1]{3,2,1,0:T(8,128)S(1)} collective-permute-done((f32[4,16,8,1]{3,2,1,0:T(8,128)S(1)}, f32[4,16,8,1]{3,2,1,0:T(8,128)S(1)}, u32[]{:S(2)}, u32[]{:S(2)}) %collective-permute-start.8) | collective-permute-done | bytes 2080 | tf_op jit(solution)/shard_map/ppermute | solution.py:19
  57.0 0.5 pad_maximum_fusion.12
  57.5 3.8 %collective-permute-start.11 = (f32[4,16,1,130]{3,2,1,0:T(1,128)S(1)}, f32[4,16,1,130]{3,2,1,0:T(1,128)S(1)}, u32[]{:S(2)}, u32[]{:S(2)}) collective-permute-start(f32[4,16,1,130]{3,2,1,0:T(1,128)S(1)} %get-tuple-element.41), channel_id=1, source_target_pairs={{1,0},{2,1},{3,2},{0,3},{5,4},{6,5},{7,6},{4,7},{9,8},{10,9},{11,1... | collective-permute-start | bytes 99848 | tf_op jit(solution)/shard_map/ppermute | solution.py:21
  61.3 2.4 collective-permute-done.10
  63.8 0.6 maximum_select_fusion.2
  64.7 2.6 collective-permute-start.13
  67.3 1.9 collective-permute-done.12
  69.4 1.8 collective-permute-start.14
  71.3 2.0 collective-permute-start.15
  73.3 1.8 collective-permute-done.14
  75.4 0.2 fusion.112
  75.6 0.9 multiply_reduce_fusion.7
  76.5 39.3 %all-reduce.45 = (f32[]{:T(128)}, f32[]{:T(128)}) all-reduce(f32[]{:T(128)} %get-tuple-element.10, f32[]{:T(128)} %get-tuple-element.9), channel_id=1, replica_groups=mesh['gx'=8,'gy'=4] {'gx','gy'}, use_global_device_ids=true, to_apply=%region_1.2 | all-reduce | flops 2 | bytes 16 | tf_op jit(solution)/shard_map/psum | solution.py:185
  117.3 2.6 collective-permute-start.17
  120.0 1.9 collective-permute-done.16
  122.1 2.2 collective-permute-start.18
  124.3 1.7 collective-permute-start.19
  126.0 1.7 collective-permute-done.18
  127.7 0.3 collective-permute-done.19
  128.4 0.9 multiply_reduce_fusion.6
  129.3 40.7 %psum.58 = f32[]{:T(128)} all-reduce(f32[]{:T(128)} %get-tuple-element.19), channel_id=1, replica_groups=mesh['gx'=8,'gy'=4] {'gx','gy'}, use_global_device_ids=true, to_apply=%region_5.6 | all-reduce | flops 1 | bytes 8 | tf_op jit(solution)/shard_map/psum | solution.py:197
  171.3 0.6 multiply_reduce_fusion.4
  171.9 41.6 %all-reduce.44 = (f32[]{:T(128)}, f32[]{:T(128)}) all-reduce(f32[]{:T(128)} %get-tuple-element.8, f32[]{:T(128)} %get-tuple-element.7), channel_id=1, replica_groups=mesh['gx'=8,'gy'=4] {'gx','gy'}, use_global_device_ids=true, to_apply=%region_7.8 | all-reduce | flops 2 | bytes 16 | tf_op jit(solution)/shard_map/psum | solution.py:205
  215.0 2.6 collective-permute-start.21
  217.6 1.9 collective-permute-done.20
  219.9 3.7 %collective-permute-start.23 = (f32[16,1,130]{2,1,0:T(1,128)S(1)}, f32[16,1,130]{2,1,0:T(1,128)S(1)}, u32[]{:S(2)}, u32[]{:S(2)}) collective-permute-start(f32[16,1,130]{2,1,0:T(1,128)S(1)} %get-tuple-element.107), channel_id=1, source_target_pairs={{1,0},{2,1},{3,2},{0,3},{5,4},{6,5},{7,6},{4,7},{9,8},{10,9},{11,1... | collective-permute-start | bytes 24968 | tf_op jit(solution)/shard_map/ppermute | solution.py:21
  223.6 1.7 collective-permute-done.22
  225.5 0.2 fusion.110
  225.7 0.9 multiply_reduce_fusion.3
  226.7 1.4 pad_maximum_fusion.29
  228.1 39.8 %psum.61 = f32[2]{0:T(128)S(1)} all-reduce(f32[2]{0:T(128)S(1)} %pad_maximum_fusion.29), channel_id=1, replica_groups=mesh['gx'=8,'gy'=4] {'gx','gy'}, use_global_device_ids=true, to_apply=%region_12.13 | all-reduce | flops 2 | bytes 16 | tf_op jit(solution)/shard_map/psum | solution.py:197
  267.8 0.6 fusion.120
  271.1 0.6 multiply_reduce_fusion
  271.7 42.2 %all-reduce.43 = (f32[]{:T(128)}, f32[]{:T(128)}) all-reduce(f32[]{:T(128)} %get-tuple-element.4, f32[]{:T(128)} %get-tuple-element.3), channel_id=1, replica_groups=mesh['gx'=8,'gy'=4] {'gx','gy'}, use_global_device_ids=true, to_apply=%region_14.15 | all-reduce | flops 2 | bytes 16 | tf_op jit(solution)/shard_map/psum | solution.py:205
  315.5 2.6 collective-permute-start.25
  318.1 0.6 slice_bitcast_fusion.8
  318.7 1.3 collective-permute-done.24
  320.3 3.8 %collective-permute-start.27 = (f32[16,1,130]{2,1,0:T(1,128)S(1)}, f32[16,1,130]{2,1,0:T(1,128)S(1)}, u32[]{:S(2)}, u32[]{:S(2)}) collective-permute-start(f32[16,1,130]{2,1,0:T(1,128)S(1)} %get-tuple-element.105), channel_id=1, source_target_pairs={{1,0},{2,1},{3,2},{0,3},{5,4},{6,5},{7,6},{4,7},{9,8},{10,9},{11,1... | collective-permute-start | bytes 24968 | tf_op jit(solution)/shard_map/ppermute | solution.py:21
  324.1 1.7 collective-permute-done.26
  326.1 0.7 pad_maximum_fusion.2
  (71 shorter events, 4.2 us)
Async XLA Ops:
  0.6 16.2 %copy-start.6 = (f32[16,8,128]{2,1,0:T(8,128)S(1)}, f32[16,8,128]{2,1,0:T(8,128)}, u32[]{:S(2)}) copy-start(f32[16,8,128]{2,1,0:T(8,128)} %param.7) | copy-start | bytes 196612
  0.6 16.2 %copy-start.5 = (f32[16,8,128]{2,1,0:T(8,128)S(1)}, f32[16,8,128]{2,1,0:T(8,128)}, u32[]{:S(2)}) copy-start(f32[16,8,128]{2,1,0:T(8,128)} %param.9) | copy-start | bytes 196612
  0.7 16.1 %copy-start.2 = (f32[3,16,8,128]{3,2,1,0:T(8,128)S(1)}, f32[3,16,8,128]{3,2,1,0:T(8,128)}, u32[]{:S(2)}) copy-start(f32[3,16,8,128]{3,2,1,0:T(8,128)} %param.6) | copy-start | bytes 589828
  0.7 16.1 %copy-start.1 = (f32[3,16,8,128]{3,2,1,0:T(8,128)S(1)}, f32[3,16,8,128]{3,2,1,0:T(8,128)}, u32[]{:S(2)}) copy-start(f32[3,16,8,128]{3,2,1,0:T(8,128)} %param.8) | copy-start | bytes 589828
  2.1 13.2 %collective-permute-start = (f32[8,16,8,1]{3,2,1,0:T(8,128)S(1)}, f32[8,16,8,1]{3,2,1,0:T(8,128)S(1)}, u32[]{:S(2)}, u32[]{:S(2)}) collective-permute-start(f32[8,16,8,1]{3,2,1,0:T(8,128)S(1)} %get-tuple-element.50), channel_id=1, source_target_pairs={{0,4},{4,8},{8,12},{12,16},{16,20},{20,24},{24,28},{28,0},{1,5},{5... | collective-permute-start | bytes 12296 | tf_op jit(solution)/shard_map/ppermute | solution.py:19
  2.6 14.2 %collective-permute-start.1 = (f32[8,16,8,1]{3,2,1,0:T(8,128)S(1)}, f32[8,16,8,1]{3,2,1,0:T(8,128)S(1)}, u32[]{:S(2)}, u32[]{:S(2)}) collective-permute-start(f32[8,16,8,1]{3,2,1,0:T(8,128)S(1)} %get-tuple-element.51), channel_id=1, source_target_pairs={{4,0},{8,4},{12,8},{16,12},{20,16},{24,20},{28,24},{0,28},{5,1},{9... | collective-permute-start | bytes 12296 | tf_op jit(solution)/shard_map/ppermute | solution.py:21
  17.7 7.5 %collective-permute-start.2 = (f32[8,16,1,130]{3,2,1,0:T(1,128)S(1)}, f32[8,16,1,130]{3,2,1,0:T(1,128)S(1)}, u32[]{:S(2)}, u32[]{:S(2)}) collective-permute-start(f32[8,16,1,130]{3,2,1,0:T(1,128)S(1)} %get-tuple-element.32), channel_id=1, source_target_pairs={{0,1},{1,2},{2,3},{3,0},{4,5},{5,6},{6,7},{7,4},{8,9},{9,10},{10,1... | collective-permute-start | bytes 199688 | tf_op jit(solution)/shard_map/ppermute | solution.py:19
  19.3 8.9 %collective-permute-start.3 = (f32[8,16,1,130]{3,2,1,0:T(1,128)S(1)}, f32[8,16,1,130]{3,2,1,0:T(1,128)S(1)}, u32[]{:S(2)}, u32[]{:S(2)}) collective-permute-start(f32[8,16,1,130]{3,2,1,0:T(1,128)S(1)} %get-tuple-element.33), channel_id=1, source_target_pairs={{1,0},{2,1},{3,2},{0,3},{5,4},{6,5},{7,6},{4,7},{9,8},{10,9},{11,1... | collective-permute-start | bytes 199688 | tf_op jit(solution)/shard_map/ppermute | solution.py:21
  30.2 13.4 %copy-start.4 = (f32[3,16,8,128]{3,2,1,0:T(8,128)S(1)}, f32[3,16,8,128]{3,2,1,0:T(8,128)}, u32[]{:S(2)}) copy-start(f32[3,16,8,128]{3,2,1,0:T(8,128)} %param.10) | copy-start | bytes 589828
  30.7 8.5 %collective-permute-start.4 = (f32[4,16,8,1]{3,2,1,0:T(8,128)S(1)}, f32[4,16,8,1]{3,2,1,0:T(8,128)S(1)}, u32[]{:S(2)}, u32[]{:S(2)}) collective-permute-start(f32[4,16,8,1]{3,2,1,0:T(8,128)S(1)} %get-tuple-element.102), channel_id=1, source_target_pairs={{0,4},{4,8},{8,12},{12,16},{16,20},{20,24},{24,28},{28,0},{1,5},{5... | collective-permute-start | bytes 6152 | tf_op jit(solution)/shard_map/ppermute | solution.py:19
  30.9 8.3 %collective-permute-start.5 = (f32[4,16,8,1]{3,2,1,0:T(8,128)S(1)}, f32[4,16,8,1]{3,2,1,0:T(8,128)S(1)}, u32[]{:S(2)}, u32[]{:S(2)}) collective-permute-start(f32[4,16,8,1]{3,2,1,0:T(8,128)S(1)} %get-tuple-element.103), channel_id=1, source_target_pairs={{4,0},{8,4},{12,8},{16,12},{20,16},{24,20},{28,24},{0,28},{5,1},{9... | collective-permute-start | bytes 6152 | tf_op jit(solution)/shard_map/ppermute | solution.py:21
  39.7 6.8 %collective-permute-start.6 = (f32[4,16,1,130]{3,2,1,0:T(1,128)S(1)}, f32[4,16,1,130]{3,2,1,0:T(1,128)S(1)}, u32[]{:S(2)}, u32[]{:S(2)}) collective-permute-start(f32[4,16,1,130]{3,2,1,0:T(1,128)S(1)} %get-tuple-element.42), channel_id=1, source_target_pairs={{0,1},{1,2},{2,3},{3,0},{4,5},{5,6},{6,7},{7,4},{8,9},{9,10},{10,1... | collective-permute-start | bytes 99848 | tf_op jit(solution)/shard_map/ppermute | solution.py:19
  40.8 6.3 %collective-permute-start.7 = (f32[4,16,1,130]{3,2,1,0:T(1,128)S(1)}, f32[4,16,1,130]{3,2,1,0:T(1,128)S(1)}, u32[]{:S(2)}, u32[]{:S(2)}) collective-permute-start(f32[4,16,1,130]{3,2,1,0:T(1,128)S(1)} %get-tuple-element.43), channel_id=1, source_target_pairs={{1,0},{2,1},{3,2},{0,3},{5,4},{6,5},{7,6},{4,7},{9,8},{10,9},{11,1... | collective-permute-start | bytes 99848 | tf_op jit(solution)/shard_map/ppermute | solution.py:21
  48.3 8.6 %collective-permute-start.8 = (f32[4,16,8,1]{3,2,1,0:T(8,128)S(1)}, f32[4,16,8,1]{3,2,1,0:T(8,128)S(1)}, u32[]{:S(2)}, u32[]{:S(2)}) collective-permute-start(f32[4,16,8,1]{3,2,1,0:T(8,128)S(1)} %get-tuple-element.83), channel_id=1, source_target_pairs={{0,4},{4,8},{8,12},{12,16},{16,20},{20,24},{24,28},{28,0},{1,5},{5... | collective-permute-start | bytes 6152 | tf_op jit(solution)/shard_map/ppermute | solution.py:19
  48.4 8.5 %collective-permute-start.9 = (f32[4,16,8,1]{3,2,1,0:T(8,128)S(1)}, f32[4,16,8,1]{3,2,1,0:T(8,128)S(1)}, u32[]{:S(2)}, u32[]{:S(2)}) collective-permute-start(f32[4,16,8,1]{3,2,1,0:T(8,128)S(1)} %get-tuple-element.84), channel_id=1, source_target_pairs={{4,0},{8,4},{12,8},{16,12},{20,16},{24,20},{28,24},{0,28},{5,1},{9... | collective-permute-start | bytes 6152 | tf_op jit(solution)/shard_map/ppermute | solution.py:21
  57.4 6.3 %collective-permute-start.10 = (f32[4,16,1,130]{3,2,1,0:T(1,128)S(1)}, f32[4,16,1,130]{3,2,1,0:T(1,128)S(1)}, u32[]{:S(2)}, u32[]{:S(2)}) collective-permute-start(f32[4,16,1,130]{3,2,1,0:T(1,128)S(1)} %get-tuple-element.40), channel_id=1, source_target_pairs={{0,1},{1,2},{2,3},{3,0},{4,5},{5,6},{6,7},{7,4},{8,9},{9,10},{10,1... | collective-permute-start | bytes 99848 | tf_op jit(solution)/shard_map/ppermute | solution.py:19
  57.5 6.3 %collective-permute-start.11 = (f32[4,16,1,130]{3,2,1,0:T(1,128)S(1)}, f32[4,16,1,130]{3,2,1,0:T(1,128)S(1)}, u32[]{:S(2)}, u32[]{:S(2)}) collective-permute-start(f32[4,16,1,130]{3,2,1,0:T(1,128)S(1)} %get-tuple-element.41), channel_id=1, source_target_pairs={{1,0},{2,1},{3,2},{0,3},{5,4},{6,5},{7,6},{4,7},{9,8},{10,9},{11,1... | collective-permute-start | bytes 99848 | tf_op jit(solution)/shard_map/ppermute | solution.py:21
  64.4 11.2 %copy-start.3 = (f32[3,16,8,128]{3,2,1,0:T(8,128)S(1)}, f32[3,16,8,128]{3,2,1,0:T(8,128)}, u32[]{:S(2)}) copy-start(f32[3,16,8,128]{3,2,1,0:T(8,128)} %param.11) | copy-start | bytes 589828
  64.7 4.6 %collective-permute-start.12 = (f32[16,8,1]{2,1,0:T(8,128)S(1)}, f32[16,8,1]{2,1,0:T(8,128)S(1)}, u32[]{:S(2)}, u32[]{:S(2)}) collective-permute-start(f32[16,8,1]{2,1,0:T(8,128)S(1)} %get-tuple-element.122), channel_id=1, source_target_pairs={{0,4},{4,8},{8,12},{12,16},{16,20},{20,24},{24,28},{28,0},{1,5},{5... | collective-permute-start | bytes 1544 | tf_op jit(solution)/shard_map/ppermute | solution.py:19
  64.7 4.6 %collective-permute-start.13 = (f32[16,8,1]{2,1,0:T(8,128)S(1)}, f32[16,8,1]{2,1,0:T(8,128)S(1)}, u32[]{:S(2)}, u32[]{:S(2)}) collective-permute-start(f32[16,8,1]{2,1,0:T(8,128)S(1)} %get-tuple-element.123), channel_id=1, source_target_pairs={{4,0},{8,4},{12,8},{16,12},{20,16},{24,20},{28,24},{0,28},{5,1},{9... | collective-permute-start | bytes 1544 | tf_op jit(solution)/shard_map/ppermute | solution.py:21
  69.4 5.7 %collective-permute-start.14 = (f32[16,1,130]{2,1,0:T(1,128)S(1)}, f32[16,1,130]{2,1,0:T(1,128)S(1)}, u32[]{:S(2)}, u32[]{:S(2)}) collective-permute-start(f32[16,1,130]{2,1,0:T(1,128)S(1)} %get-tuple-element.112), channel_id=1, source_target_pairs={{0,1},{1,2},{2,3},{3,0},{4,5},{5,6},{6,7},{7,4},{8,9},{9,10},{10,1... | collective-permute-start | bytes 24968 | tf_op jit(solution)/shard_map/ppermute | solution.py:19
  71.3 3.9 %collective-permute-start.15 = (f32[16,1,130]{2,1,0:T(1,128)S(1)}, f32[16,1,130]{2,1,0:T(1,128)S(1)}, u32[]{:S(2)}, u32[]{:S(2)}) collective-permute-start(f32[16,1,130]{2,1,0:T(1,128)S(1)} %get-tuple-element.113), channel_id=1, source_target_pairs={{1,0},{2,1},{3,2},{0,3},{5,4},{6,5},{7,6},{4,7},{9,8},{10,9},{11,1... | collective-permute-start | bytes 24968 | tf_op jit(solution)/shard_map/ppermute | solution.py:21
  117.3 4.6 %collective-permute-start.16 = (f32[16,8,1]{2,1,0:T(8,128)S(1)}, f32[16,8,1]{2,1,0:T(8,128)S(1)}, u32[]{:S(2)}, u32[]{:S(2)}) collective-permute-start(f32[16,8,1]{2,1,0:T(8,128)S(1)} %get-tuple-element.120), channel_id=1, source_target_pairs={{0,4},{4,8},{8,12},{12,16},{16,20},{20,24},{24,28},{28,0},{1,5},{5... | collective-permute-start | bytes 1544 | tf_op jit(solution)/shard_map/ppermute | solution.py:19
  117.3 4.6 %collective-permute-start.17 = (f32[16,8,1]{2,1,0:T(8,128)S(1)}, f32[16,8,1]{2,1,0:T(8,128)S(1)}, u32[]{:S(2)}, u32[]{:S(2)}) collective-permute-start(f32[16,8,1]{2,1,0:T(8,128)S(1)} %get-tuple-element.121), channel_id=1, source_target_pairs={{4,0},{8,4},{12,8},{16,12},{20,16},{24,20},{28,24},{0,28},{5,1},{9... | collective-permute-start | bytes 1544 | tf_op jit(solution)/shard_map/ppermute | solution.py:21
  122.1 5.6 %collective-permute-start.18 = (f32[16,1,130]{2,1,0:T(1,128)S(1)}, f32[16,1,130]{2,1,0:T(1,128)S(1)}, u32[]{:S(2)}, u32[]{:S(2)}) collective-permute-start(f32[16,1,130]{2,1,0:T(1,128)S(1)} %get-tuple-element.108), channel_id=1, source_target_pairs={{0,1},{1,2},{2,3},{3,0},{4,5},{5,6},{6,7},{7,4},{8,9},{9,10},{10,1... | collective-permute-start | bytes 24968 | tf_op jit(solution)/shard_map/ppermute | solution.py:19
  124.3 3.7 %collective-permute-start.19 = (f32[16,1,130]{2,1,0:T(1,128)S(1)}, f32[16,1,130]{2,1,0:T(1,128)S(1)}, u32[]{:S(2)}, u32[]{:S(2)}) collective-permute-start(f32[16,1,130]{2,1,0:T(1,128)S(1)} %get-tuple-element.109), channel_id=1, source_target_pairs={{1,0},{2,1},{3,2},{0,3},{5,4},{6,5},{7,6},{4,7},{9,8},{10,9},{11,1... | collective-permute-start | bytes 24968 | tf_op jit(solution)/shard_map/ppermute | solution.py:21
  215.0 4.6 %collective-permute-start.20 = (f32[16,8,1]{2,1,0:T(8,128)S(1)}, f32[16,8,1]{2,1,0:T(8,128)S(1)}, u32[]{:S(2)}, u32[]{:S(2)}) collective-permute-start(f32[16,8,1]{2,1,0:T(8,128)S(1)} %get-tuple-element.118), channel_id=1, source_target_pairs={{0,4},{4,8},{8,12},{12,16},{16,20},{20,24},{24,28},{28,0},{1,5},{5... | collective-permute-start | bytes 1544 | tf_op jit(solution)/shard_map/ppermute | solution.py:19
  215.0 4.6 %collective-permute-start.21 = (f32[16,8,1]{2,1,0:T(8,128)S(1)}, f32[16,8,1]{2,1,0:T(8,128)S(1)}, u32[]{:S(2)}, u32[]{:S(2)}) collective-permute-start(f32[16,8,1]{2,1,0:T(8,128)S(1)} %get-tuple-element.119), channel_id=1, source_target_pairs={{4,0},{8,4},{12,8},{16,12},{20,16},{24,20},{28,24},{0,28},{5,1},{9... | collective-permute-start | bytes 1544 | tf_op jit(solution)/shard_map/ppermute | solution.py:21
  219.8 5.6 %collective-permute-start.22 = (f32[16,1,130]{2,1,0:T(1,128)S(1)}, f32[16,1,130]{2,1,0:T(1,128)S(1)}, u32[]{:S(2)}, u32[]{:S(2)}) collective-permute-start(f32[16,1,130]{2,1,0:T(1,128)S(1)} %get-tuple-element.106), channel_id=1, source_target_pairs={{0,1},{1,2},{2,3},{3,0},{4,5},{5,6},{6,7},{7,4},{8,9},{9,10},{10,1... | collective-permute-start | bytes 24968 | tf_op jit(solution)/shard_map/ppermute | solution.py:19
  219.9 5.5 %collective-permute-start.23 = (f32[16,1,130]{2,1,0:T(1,128)S(1)}, f32[16,1,130]{2,1,0:T(1,128)S(1)}, u32[]{:S(2)}, u32[]{:S(2)}) collective-permute-start(f32[16,1,130]{2,1,0:T(1,128)S(1)} %get-tuple-element.107), channel_id=1, source_target_pairs={{1,0},{2,1},{3,2},{0,3},{5,4},{6,5},{7,6},{4,7},{9,8},{10,9},{11,1... | collective-permute-start | bytes 24968 | tf_op jit(solution)/shard_map/ppermute | solution.py:21
  315.3 11.5 %copy-start = (f32[16,8,128]{2,1,0:T(8,128)}, f32[16,8,128]{2,1,0:T(8,128)S(1)}, u32[]{:S(2)}) copy-start(f32[16,8,128]{2,1,0:T(8,128)S(1)} %multiply_add_fusion) | copy-start | bytes 196612
  315.4 4.6 %collective-permute-start.24 = (f32[16,8,1]{2,1,0:T(8,128)S(1)}, f32[16,8,1]{2,1,0:T(8,128)S(1)}, u32[]{:S(2)}, u32[]{:S(2)}) collective-permute-start(f32[16,8,1]{2,1,0:T(8,128)S(1)} %get-tuple-element.114), channel_id=1, source_target_pairs={{0,4},{4,8},{8,12},{12,16},{16,20},{20,24},{24,28},{28,0},{1,5},{5... | collective-permute-start | bytes 1544 | tf_op jit(solution)/shard_map/ppermute | solution.py:19
  315.5 4.6 %collective-permute-start.25 = (f32[16,8,1]{2,1,0:T(8,128)S(1)}, f32[16,8,1]{2,1,0:T(8,128)S(1)}, u32[]{:S(2)}, u32[]{:S(2)}) collective-permute-start(f32[16,8,1]{2,1,0:T(8,128)S(1)} %get-tuple-element.115), channel_id=1, source_target_pairs={{4,0},{8,4},{12,8},{16,12},{20,16},{24,20},{28,24},{0,28},{5,1},{9... | collective-permute-start | bytes 1544 | tf_op jit(solution)/shard_map/ppermute | solution.py:21
  320.2 5.6 %collective-permute-start.26 = (f32[16,1,130]{2,1,0:T(1,128)S(1)}, f32[16,1,130]{2,1,0:T(1,128)S(1)}, u32[]{:S(2)}, u32[]{:S(2)}) collective-permute-start(f32[16,1,130]{2,1,0:T(1,128)S(1)} %get-tuple-element.104), channel_id=1, source_target_pairs={{0,1},{1,2},{2,3},{3,0},{4,5},{5,6},{6,7},{7,4},{8,9},{9,10},{10,1... | collective-permute-start | bytes 24968 | tf_op jit(solution)/shard_map/ppermute | solution.py:19
  320.3 5.5 %collective-permute-start.27 = (f32[16,1,130]{2,1,0:T(1,128)S(1)}, f32[16,1,130]{2,1,0:T(1,128)S(1)}, u32[]{:S(2)}, u32[]{:S(2)}) collective-permute-start(f32[16,1,130]{2,1,0:T(1,128)S(1)} %get-tuple-element.105), channel_id=1, source_target_pairs={{1,0},{2,1},{3,2},{0,3},{5,4},{6,5},{7,6},{4,7},{9,8},{10,9},{11,1... | collective-permute-start | bytes 24968 | tf_op jit(solution)/shard_map/ppermute | solution.py:21
where the time goes:
time: 328 us; the launch traced here: 327 us
  blocking collectives  204 us (62%)
  waiting for transfers between devices  50 us (15%)
  starting transfers between devices  46.6 us (14%)
  other arithmetic  14.3 us (4%)
  between operations  9.08 us (3%)
    psum x2, blocking collectives, local(): lax.psum((jnp.sum(resid * new_img), jnp.sum(new_img * new_img)), ('gx', '...  83.8 us
    psum x2, blocking collectives, local(): totals = lax.psum(locals_proj, ('gx', 'gy'))  80.5 us
    ppermute x14, waiting for transfers between devices, extended(): lax.ppermute(tail, axis, [(i, (i + 1) % count) for i in range(count)])  44.5 us
    psum x1, blocking collectives, local(): lax.psum((jnp.sum(resid * images[0]), jnp.sum(images[0] * images[0])), ('...  39.3 us
    ppermute x14, starting transfers between devices, extended(): lax.ppermute(head, axis, [((i + 1) % count, i) for i in range(count)])  38.7 us
    ppermute x14, starting transfers between devices, extended(): lax.ppermute(tail, axis, [(i, (i + 1) % count) for i in range(count)])  7.92 us
  transfers between devices with their start and end apart: 28, of which 19 were waited for; matrix products, arithmetic and copies ran while one was open for 0% of the time, Pallas kernels for 0%

commit v1 on v0

v1 whole, which is shorter than its diff:
```python
import functools

import jax
import jax.numpy as jnp
from jax import lax
from jax.experimental import pallas as pl
from jax.experimental.pallas import tpu as pltpu
from jax.sharding import PartitionSpec as P

ITERS = 3
HELM = 0.02
SHIFT = 6.0
MESH = pl.DeviceIdType.MESH

ORDER = (1, 5, 7, 0, 2, 4, 6, 9, 8, 10, 11, 12, 13, 3)
V, CY, RHO, U, W, CX, CZ, A22, A11, A33, A12, A13, A23, TH = range(14)
HALF = 7
THIRD = (2, 1)


def kernel(nx, ny, mom, theta, cour, dens, diag, cross, mom_out, th_out, p_out,
           cells, rows, edges, packed, beside, corner, first, second, coef,
           kry, rhs_rows, rhs_edges, rhs_packed, rhs_beside, rhs_corner,
           part, part_x, sum_x, part_y, in_sem, send_sem, recv_sem):
    gx = lax.axis_index("gx")
    gy = lax.axis_index("gy")
    nz = rows.shape[2]
    ny_dev = 8
    plane = nz * ny_dev

    def device(dx, dy):
        return {"gx": lax.rem(gx + dx + nx, nx), "gy": gy + dy}

    barrier = pltpu.get_barrier_semaphore()
    peers = [(lax.rem(gx + d, nx), gy) for d in range(1, nx)]
    peers += [(gx, lax.rem(gy + d, ny)) for d in range(1, ny)]
    peers += [(lax.rem(gx + a, nx), lax.rem(gy + b, ny)) for a in (1, nx - 1) for b in (1, ny - 1)]
    for a, b in peers:
        pl.semaphore_signal(barrier, inc=1, device_id={"gx": a, "gy": b}, device_id_type=MESH)

    loads = []
    place = 0
    for n, ref in enumerate((mom, theta, cour, dens, diag, cross)):
        size = ref.shape[0]
        loads.append(pltpu.make_async_copy(ref, cells.at[pl.ds(place, size)], in_sem.at[n]))
        place += size
    for n in (0, 2, 3, 1, 4, 5):
        loads[n].start()

    def clear(lo):
        rows[lo:lo + 3] = jnp.zeros((3,) + rows.shape[1:], jnp.float32)
        edges[lo:lo + 3] = jnp.zeros((3,) + edges.shape[1:], jnp.float32)
        for i in range(lo, lo + 3):
            rows[i, RHO] = jnp.ones(rows.shape[2:], jnp.float32)
            edges[i, RHO] = jnp.ones(rows.shape[2:], jnp.float32)
        rhs_rows[lo:lo + 3] = jnp.zeros((3,) + rhs_rows.shape[1:], jnp.float32)
        rhs_edges[lo:lo + 3] = jnp.zeros((3,) + rhs_edges.shape[1:], jnp.float32)

    pl.when(gy == 0)(lambda: clear(0))
    pl.when(gy == ny - 1)(lambda: clear(11))

    lane = lax.broadcasted_iota(jnp.int32, (nz, 128), 1)
    level = lax.broadcasted_iota(jnp.int32, (nz, 128), 0)
    slot = lane // 8
    from_left = lax.rem(lane, 8) < 4
    wide_level = lax.broadcasted_iota(jnp.int32, (nz, 256), 0)
    last = wide_level == nz - 1
    ground = wide_level == 0

    def xm(a):
        return pltpu.roll(a, 1, 1)

    def xp(a):
        return pltpu.roll(a, 255, 1)

    def zp(a):
        return jnp.where(last, 0.0, pltpu.roll(a, nz - 1, 0))

    def zm(a):
        return jnp.where(ground, 0.0, pltpu.roll(a, 1, 0))

    def load_half(b):
        def one(j, _):
            for f in range(b * HALF, b * HALF + HALF):
                value = cells[pl.ds(ORDER[f] * plane + j, nz, stride=ny_dev), :]
                if f == CY:
                    value = jnp.where(gy * ny_dev + j == 0, 0.0, value)
                if f == CZ:
                    value = jnp.where(level == 0, 0.0, value)
                rows[3 + j, f] = value
            return 0
        lax.fori_loop(0, ny_dev, one, 0)

    def pack_half(b):
        def one(t, _):
            acc = jnp.zeros((nz, 128), jnp.float32)
            for side in range(2):
                for fi in range(HALF):
                    p = 64 * side + 8 * fi
                    moved = pltpu.roll(rows[3 + 2 * t + side, b * HALF + fi], (p + 4) % 128, 1)
                    acc = jnp.where(slot == p // 8, moved, acc)
            packed[b, t] = acc
            return 0
        lax.fori_loop(0, ny_dev // 2, one, 0)

    def unpack_half(b):
        def spread(tile, side, row, count):
            for fi in range(count):
                p = 64 * side + 8 * fi
                edges[row, b * HALF + fi] = pltpu.roll(tile, (128 - (p + 4)) % 128, 1)

        def one(t, _):
            tile = jnp.where(from_left, beside[b, 0, t], beside[b, 1, t])
            for side in range(2):
                spread(tile, side, 3 + 2 * t + side, HALF)
            return 0
        lax.fori_loop(0, ny_dev // 2, one, 0)

        @pl.when(gy > 0)
        def _():
            for j in (5, 6, 7):
                tile = jnp.where(from_left, corner[b, 0, 0, j // 2 - 2], corner[b, 0, 1, j // 2 - 2])
                spread(tile, j % 2, j - 5, THIRD[b] if j == 5 else HALF)

        @pl.when(gy < ny - 1)
        def _():
            for j in (0, 1, 2):
                tile = jnp.where(from_left, corner[b, 1, 0, j // 2], corner[b, 1, 1, j // 2])
                spread(tile, j % 2, 11 + j, THIRD[b] if j == 2 else HALF)

    def remote(src, dst, k, dx, dy):
        return pltpu.make_async_remote_copy(
            src_ref=src, dst_ref=dst, send_sem=send_sem.at[k], recv_sem=recv_sem.at[k],
            device_id=device(dx, dy), device_id_type=MESH)

    def group(entries, base):
        by = {1: [], -1: [], 0: []}
        for n, (dx, dy, src, dst) in enumerate(entries):
            by[dy].append((src, dst, base + n, dx, dy))
        return by

    def each(by, action, sign):
        for dy in (1, -1, 0):
            def run(dy=dy):
                for item in by[dy]:
                    action(remote(*item))
            if dy == 0:
                run()
            elif dy * sign == 1:
                pl.when(gy < ny - 1)(run)
            else:
                pl.when(gy > 0)(run)

    def start(by):
        each(by, lambda c: c.start(), 1)

    def wait_recv(by):
        each(by, lambda c: c.wait_recv(), -1)

    def wait_send(by):
        each(by, lambda c: c.wait_send(), 1)

    def half_entries(b):
        fs = pl.ds(b * HALF, HALF)
        ft = pl.ds(b * HALF, THIRD[b])
        return [
            (0, 1, rows.at[pl.ds(9, 2), fs], rows.at[pl.ds(1, 2), fs]),
            (0, 1, rows.at[pl.ds(8, 1), ft], rows.at[pl.ds(0, 1), ft]),
            (0, -1, rows.at[pl.ds(3, 2), fs], rows.at[pl.ds(11, 2), fs]),
            (0, -1, rows.at[pl.ds(5, 1), ft], rows.at[pl.ds(13, 1), ft]),
            (1, 0, packed.at[b], beside.at[b, 0]),
            (-1, 0, packed.at[b], beside.at[b, 1]),
            (1, 1, packed.at[b, pl.ds(2, 2)], corner.at[b, 0, 0]),
            (-1, 1, packed.at[b, pl.ds(2, 2)], corner.at[b, 0, 1]),
            (1, -1, packed.at[b, pl.ds(0, 2)], corner.at[b, 1, 0]),
            (-1, -1, packed.at[b, pl.ds(0, 2)], corner.at[b, 1, 1]),
        ]

    half_a = group(half_entries(0), 0)
    half_b = group(half_entries(1), 10)
    half_r = group([
        (0, 1, rhs_rows.at[pl.ds(8, 3)], rhs_rows.at[pl.ds(0, 3)]),
        (0, -1, rhs_rows.at[pl.ds(3, 3)], rhs_rows.at[pl.ds(11, 3)]),
        (1, 0, rhs_packed, rhs_beside.at[0]),
        (-1, 0, rhs_packed, rhs_beside.at[1]),
        (1, 1, rhs_packed, rhs_corner.at[0, 0]),
        (-1, 1, rhs_packed, rhs_corner.at[0, 1]),
        (1, -1, rhs_packed, rhs_corner.at[1, 0]),
        (-1, -1, rhs_packed, rhs_corner.at[1, 1]),
    ], 20)

    for n in (0, 2, 3):
        loads[n].wait()
    load_half(0)
    pack_half(0)
    pl.semaphore_wait(barrier, len(peers))
    start(half_a)
    for n in (1, 4, 5):
        loads[n].wait()
    load_half(1)
    pack_half(1)
    start(half_b)

    def wide(r, f):
        return jnp.concatenate([rows[r, f], edges[r, f]], axis=1)

    def upwind(fields, lo, hi):
        def one(r, _):
            cx, cy, cy_up, cz = wide(r, CX), wide(r, CY), wide(r + 1, CY), wide(r, CZ)
            inv = 1.0 / wide(r, RHO)
            cx_p, cx_n = jnp.maximum(cx, 0.0), jnp.minimum(cx, 0.0)
            cy_p, cy_n = jnp.maximum(cy, 0.0), jnp.minimum(cy, 0.0)
            cu_p, cu_n = jnp.maximum(cy_up, 0.0), jnp.minimum(cy_up, 0.0)
            cz_p, cz_n = jnp.maximum(cz, 0.0), jnp.minimum(cz, 0.0)
            for n, f in fields:
                here = wide(r, f)
                fx = cx_p * xm(here) + cx_n * here
                fz = cz_p * zm(here) + cz_n * here
                fy = cy_p * wide(r - 1, f) + cy_n * here
                fu = cu_p * here + cu_n * wide(r + 1, f)
                total = xp(fx) - fx + fu - fy + zp(fz) - fz
                first[r, n] = here - total * inv
            return 0
        lax.fori_loop(lo, hi, one, 0)

    def antidiffuse(fields, lo, hi):
        def one(r, _):
            cx, cy, cy_up, cz = wide(r, CX), wide(r, CY), wide(r + 1, CY), wide(r, CZ)
            rho = wide(r, RHO)
            inv = 1.0 / rho

            def face(c, a, b):
                return 0.5 * jnp.abs(c) - c * c / (a + b)

            kx = face(cx, xm(rho), rho)
            ky = face(cy, wide(r - 1, RHO), rho)
            ku = face(cy_up, rho, wide(r + 1, RHO))
            kz = face(cz, zm(rho), rho)
            for n in fields:
                here = first[r, n]
                ax = kx * (here - xm(here))
                az = kz * (here - zm(here))
                ay = ky * (here - first[r - 1, n])
                au = ku * (first[r + 1, n] - here)
                total = xp(ax) - ax + au - ay + zp(az) - az
                second[r, n] = here - total * inv
            return 0
        lax.fori_loop(lo, hi, one, 0)

    wait_recv(half_a)
    unpack_half(0)
    upwind(((0, U), (1, V), (2, W)), 1, 13)
    antidiffuse((0, 1, 2), 2, 12)

    def make_rhs(j, acc):
        r = 3 + j
        u, w = second[r, 0], second[r, 2]
        value = (0.5 * (xp(u) - xm(u)) + 0.5 * (second[r + 1, 1] - second[r - 1, 1])
                 + 0.5 * (zp(w) - zm(w)))[:, :128]
        rhs_rows[r] = value
        return jnp.where(slot == j, pltpu.roll(value, 8 * j + 4, 1), acc)

    rhs_packed[...] = lax.fori_loop(0, ny_dev, make_rhs, jnp.zeros((nz, 128), jnp.float32))
    start(half_r)

    wait_recv(half_b)
    unpack_half(1)

    def make_coef(r, _):
        a11, a22, a33 = wide(r, A11), wide(r, A22), wide(r, A33)
        at = gy * ny_dev + r - 3
        wxl = 0.5 * (xm(a11) + a11)
        wx = xp(wxl)
        wyl = jnp.where((at > 0) & (at < ny * ny_dev), 0.5 * (wide(r - 1, A22) + a22), 0.0)
        wy = jnp.where((at > -1) & (at < ny * ny_dev - 1), 0.5 * (a22 + wide(r + 1, A22)), 0.0)
        wzl = jnp.where(ground, 0.0, 0.5 * (zm(a33) + a33))
        wz = zp(wzl)
        coef[r, 0] = wx
        coef[r, 1] = wxl
        coef[r, 2] = wy
        coef[r, 3] = wyl
        coef[r, 4] = wz
        coef[r, 5] = wzl
        coef[r, 6] = (SHIFT - HELM) - (wx + wxl + wy + wyl + wz + wzl)
        coef[r, 7] = 0.25 * wide(r, A12)
        coef[r, 8] = 0.25 * wide(r, A13)
        coef[r, 9] = 0.25 * wide(r, A23)
        return 0

    lax.fori_loop(1, 13, make_coef, 0)

    wait_recv(half_r)

    def spread_rhs(j, tile, row):
        edge = pltpu.roll(tile, 128 - (8 * j + 4), 1)
        kry[0, row] = jnp.concatenate([rhs_rows[row], edge], axis=1)

    tile = jnp.where(from_left, rhs_beside[0], rhs_beside[1])
    for j in range(ny_dev):
        spread_rhs(j, tile, 3 + j)

    def halo_rhs(side, js, lo, inside):
        @pl.when(inside)
        def _():
            tile = jnp.where(from_left, rhs_corner[side, 0], rhs_corner[side, 1])
            for n, j in enumerate(js):
                spread_rhs(j, tile, lo + n)

        @pl.when(jnp.logical_not(inside))
        def _():
            for n in range(3):
                kry[0, lo + n] = jnp.zeros((nz, 256), jnp.float32)

    halo_rhs(0, (5, 6, 7), 0, gy > 0)
    halo_rhs(1, (0, 1, 2), 11, gy < ny - 1)

    def operate(n, r):
        p, up, down = kry[n, r], kry[n, r + 1], kry[n, r - 1]
        right, left = xp(p), xm(p)
        dx = right - left
        dy = up - down
        return (coef[r, 0] * right + coef[r, 1] * left + coef[r, 2] * up + coef[r, 3] * down
                + coef[r, 4] * zp(p) + coef[r, 5] * zm(p) + coef[r, 6] * p
                + coef[r, 7] * ((xp(up) - xm(up)) - (xp(down) - xm(down)))
                + coef[r, 8] * (zp(dx) - zm(dx)) + coef[r, 9] * (zp(dy) - zm(dy)))

    for n in range(2):
        def lift(r, _, n=n):
            kry[n + 1, r] = operate(n, r)
            return 0
        lax.fori_loop(1 + n, 13 - n, lift, 0)

    pairs = [(a, b) for a in range(ITERS + 1) for b in range(a, ITERS + 1)]

    def gram(r, acc):
        vecs = [kry[n, r][:, :128] for n in range(ITERS)] + [operate(ITERS - 1, r)[:, :128]]
        out = []
        for (a, b), s in zip(pairs, acc):
            prod = vecs[a] * vecs[b]
            out.append(s + (prod[:8] + prod[8:]))
        return tuple(out)

    sums = lax.fori_loop(3, 3 + ny_dev, gram, tuple(jnp.zeros((8, 128), jnp.float32) for _ in pairs))
    spot = lax.broadcasted_iota(jnp.int32, (16, 128), 0)
    tile = jnp.zeros((16, 128), jnp.float32)
    for n, s in enumerate(sums):
        tile = jnp.where(spot == n, jnp.sum(s, axis=0, keepdims=True), tile)
    part[...] = tile

    def x_copy(d):
        k = 28 + d - 1
        return pltpu.make_async_remote_copy(
            src_ref=part, dst_ref=part_x.at[d - 1], send_sem=send_sem.at[k], recv_sem=recv_sem.at[k],
            device_id={"gx": lax.rem(gx + d, nx), "gy": gy}, device_id_type=MESH)

    def y_copy(d):
        k = 28 + nx - 1 + d - 1
        return pltpu.make_async_remote_copy(
            src_ref=sum_x, dst_ref=part_y.at[d - 1], send_sem=send_sem.at[k], recv_sem=recv_sem.at[k],
            device_id={"gx": gx, "gy": lax.rem(gy + d, ny)}, device_id_type=MESH)

    for d in range(1, nx):
        x_copy(d).start()
    upwind(((3, TH),), 2, 12)
    for d in range(1, nx):
        x_copy(d).wait_recv()
    tile = part[...]
    for d in range(1, nx):
        tile = tile + part_x[d - 1]
    sum_x[...] = tile
    for d in range(1, ny):
        y_copy(d).start()
    antidiffuse((3,), 3, 11)

    def store(ref, base, j, value):
        ref[pl.ds(base + j, nz, stride=ny_dev), :] = value

    def put_theta(j, _):
        store(th_out, 0, j, second[3 + j, 3][:, :128])
        return 0

    lax.fori_loop(0, ny_dev, put_theta, 0)
    for d in range(1, ny):
        y_copy(d).wait_recv()
    tile = sum_x[...]
    for d in range(1, ny):
        tile = tile + part_y[d - 1]
    total = jnp.sum(tile, axis=1, keepdims=True)
    gmat = {}
    for n, (a, b) in enumerate(pairs):
        gmat[a, b] = gmat[b, a] = total[n:n + 1, :]

    def dot(a, b):
        terms = [x * y for x, y in zip(a, b) if x is not None and y is not None]
        return functools.reduce(lambda s, t: s + t, terms)

    def minus(a, s, b):
        out = []
        for x, y in zip(a, b):
            if y is None:
                out.append(x)
            else:
                out.append(-(s * y) if x is None else x - s * y)
        return out

    def image(a):
        out = [None if x is None else -SHIFT * x for x in a]
        for n in range(ITERS):
            if a[n] is not None:
                out[n + 1] = a[n] if out[n + 1] is None else out[n + 1] + a[n]
        return out

    one = jnp.ones((1, 1), jnp.float32)
    resid = [one] + [None] * ITERS
    dirs, images, duals, norms = [resid], [image(resid)], [], []
    press = [None] * (ITERS + 1)
    for step in range(ITERS):
        q = images[step]
        dual = [dot([gmat[a, b] for b in range(ITERS + 1)], q) for a in range(ITERS + 1)]
        duals.append(dual)
        norms.append(dot(q, dual))
        beta = dot(resid, dual) / norms[step]
        press = minus(press, -beta, dirs[step])
        if step + 1 < ITERS:
            resid = minus(resid, beta, q)
            lifted = image(resid)
            new_dir, new_img = resid, lifted
            for back in range(step + 1):
                alpha = dot(lifted, duals[back]) / norms[back]
                new_dir = minus(new_dir, alpha, dirs[back])
                new_img = minus(new_img, alpha, images[back])
            dirs.append(new_dir)
            images.append(new_img)
    c0, c1, c2 = [jnp.broadcast_to(c, (nz, 256)) for c in press[:ITERS]]

    def pressure(r):
        return c0 * kry[0, r] + c1 * kry[1, r] + c2 * kry[2, r]

    def finish(j, carry):
        down, here = carry
        r = 3 + j
        up = pressure(r + 1)
        store(p_out, 0, j, here[:, :128])
        store(mom_out, 0, j, (second[r, 0] - 0.5 * (xp(here) - xm(here)))[:, :128])
        store(mom_out, plane, j, (second[r, 1] - 0.5 * (up - down))[:, :128])
        store(mom_out, 2 * plane, j, (second[r, 2] - 0.5 * (zp(here) - zm(here)))[:, :128])
        return here, up

    lax.fori_loop(0, ny_dev, finish, (pressure(2), pressure(3)))

    wait_send(half_a)
    wait_send(half_b)
    wait_send(half_r)
    for d in range(1, nx):
        x_copy(d).wait_send()
    for d in range(1, ny):
        y_copy(d).wait_send()


def solution(mesh):
    nx, ny = mesh.shape["gx"], mesh.shape["gy"]

    def local(momenta, theta, courant, density, metric_diag, metric_cross):
        nz, ny_dev, nx_dev = density.shape
        args = (momenta, theta, courant, density, metric_diag, metric_cross)
        flat = [a.reshape(-1, nx_dev) for a in args]
        plane = nz * ny_dev
        f32 = jnp.float32
        n_ext = ny_dev + 6
        n_sem = 28 + nx - 1 + ny - 1
        shape = jax.ShapeDtypeStruct
        vmem = pltpu.VMEM
        mom, th, press = pl.pallas_call(
            functools.partial(kernel, nx, ny),
            out_shape=(shape((3 * plane, nx_dev), f32), shape((plane, nx_dev), f32),
                       shape((plane, nx_dev), f32)),
            in_specs=[pl.BlockSpec(memory_space=pl.ANY)] * 6,
            out_specs=[pl.BlockSpec(memory_space=pltpu.VMEM)] * 3,
            scratch_shapes=[
                vmem((14 * plane, nx_dev), f32),
                vmem((n_ext, 14, nz, nx_dev), f32),
                vmem((n_ext, 14, nz, nx_dev), f32),
                vmem((2, 4, nz, nx_dev), f32),
                vmem((2, 2, 4, nz, nx_dev), f32),
                vmem((2, 2, 2, 2, nz, nx_dev), f32),
                vmem((n_ext, 4, nz, 2 * nx_dev), f32),
                vmem((n_ext, 4, nz, 2 * nx_dev), f32),
                vmem((n_ext, 10, nz, 2 * nx_dev), f32),
                vmem((3, n_ext, nz, 2 * nx_dev), f32),
                vmem((n_ext, nz, nx_dev), f32),
                vmem((n_ext, nz, nx_dev), f32),
                vmem((nz, nx_dev), f32),
                vmem((2, nz, nx_dev), f32),
                vmem((2, 2, nz, nx_dev), f32),
                vmem((16, 128), f32),
                vmem((nx - 1, 16, 128), f32),
                vmem((16, 128), f32),
                vmem((ny - 1, 16, 128), f32),
                pltpu.SemaphoreType.DMA((6,)),
                pltpu.SemaphoreType.DMA((n_sem,)),
                pltpu.SemaphoreType.DMA((n_sem,)),
            ],
            compiler_params=pltpu.CompilerParams(
                collective_id=0, has_side_effects=True, vmem_limit_bytes=40 * 1024 * 1024),
        )(*flat)
        return mom.reshape(momenta.shape), th.reshape(theta.shape), press.reshape(theta.shape)

    placed = (
        P(None, None, "gy", "gx"),
        P(None, "gy", "gx"),
        P(None, None, "gy", "gx"),
        P(None, "gy", "gx"),
        P(None, None, "gy", "gx"),
        P(None, None, "gy", "gx"),
    )
    return jax.shard_map(
        local,
        mesh=mesh,
        in_specs=placed,
        out_specs=(P(None, None, "gy", "gx"), P(None, "gy", "gx"), P(None, "gy", "gx")),
        check_vma=False,
    )
```

time: 328 us -> 40.5 us (0.12)
  blocking collectives: 204 us -> 0 us
  waiting for transfers between devices: 50 us -> 0 us
  starting transfers between devices: 46.6 us -> 0 us
  Pallas kernels: 0 us -> 32.2 us
  other arithmetic: 14.3 us -> 0 us
  between operations: 9.08 us -> 0.65 us
  local copies, waits for them, and re-layouts: 3.21 us -> 7.31 us
    psum x5 -> x0, blocking collectives: 204 us -> none  [the longest x2 83.8 us: local(): lax.psum((jnp.sum(resid * new_img), jnp.sum(new_img * new_img)), ('gx', '...]
    ppermute x28 -> x0, waiting for transfers between devices: 50 us -> none  [the longest x14 44.5 us: extended(): lax.ppermute(tail, axis, [(i, (i + 1) % count) for i in range(count)])]
    ppermute x28 -> x0, starting transfers between devices: 46.6 us -> none  [the longest x14 38.7 us: extended(): lax.ppermute(head, axis, [((i + 1) % count, i) for i in range(count)])]
    pallas_call x0 -> x1, Pallas kernels: none -> 32.2 us  [local(): pl.pallas_call(functools.partial(kernel, nx, ny), out_shape=(shape((3 * p...]
    unnamed x14 -> x15, local copies, waits for them, and re-layouts: 0.04 us -> 7.31 us
    reduce_sum x5 -> x0, other arithmetic: 4 us -> none  [the longest x2 1.82 us: local(): locals_proj = jnp.stack([jnp.sum(lifted * image) for image in images])]
  transfers between devices with their start and end apart: 28 -> 0, of which waited for: 19 -> 0; matrix products, arithmetic and copies ran while one was open for 0% -> 0% of each run, Pallas kernels for 0% -> 0%
where the time goes in v1:
time: 40.5 us; the launch traced here: 40.2 us
  Pallas kernels  32.2 us (80%)
  local copies, waits for them, and re-layouts  7.31 us (18%)
  between operations  0.65 us (2%)
    pallas_call x1, Pallas kernels, local(): pl.pallas_call(functools.partial(kernel, nx, ny), out_shape=(shape((3 * p...  32.2 us
    unnamed x15, local copies, waits for them, and re-layouts  7.31 us

profile of v1, /device:TPU:0, one launch (start us, length us, event | category | flops | bytes accessed | tf_op | source)
XLA Modules:
  0.0 40.2 jit_solution(11831398867598148208)
XLA Ops:
  0.6 0.0 copy-start
  0.6 0.9 %copy-done = f32[3,16,8,128]{3,2,1,0:T(8,128)S(1)} copy-done((f32[3,16,8,128]{3,2,1,0:T(8,128)S(1)}, f32[3,16,8,128]{3,2,1,0:T(8,128)}, u32[]{:S(2)}) %copy-start) | copy-done | bytes 196632
  1.6 0.0 copy-start.1
  1.6 0.9 %copy-done.1 = f32[3,16,8,128]{3,2,1,0:T(8,128)S(1)} copy-done((f32[3,16,8,128]{3,2,1,0:T(8,128)S(1)}, f32[3,16,8,128]{3,2,1,0:T(8,128)}, u32[]{:S(2)}) %copy-start.1) | copy-done | bytes 196632
  2.5 0.0 copy-start.2
  2.5 0.9 %copy-done.2 = f32[3,16,8,128]{3,2,1,0:T(8,128)S(1)} copy-done((f32[3,16,8,128]{3,2,1,0:T(8,128)S(1)}, f32[3,16,8,128]{3,2,1,0:T(8,128)}, u32[]{:S(2)}) %copy-start.2) | copy-done | bytes 196632
  3.4 0.0 copy-start.3
  3.4 0.9 %copy-done.3 = f32[3,16,8,128]{3,2,1,0:T(8,128)S(1)} copy-done((f32[3,16,8,128]{3,2,1,0:T(8,128)S(1)}, f32[3,16,8,128]{3,2,1,0:T(8,128)}, u32[]{:S(2)}) %copy-start.3) | copy-done | bytes 196632
  4.3 0.0 copy-start.4
  4.3 0.8 %copy-done.4 = f32[16,8,128]{2,1,0:T(8,128)S(1)} copy-done((f32[16,8,128]{2,1,0:T(8,128)S(1)}, f32[16,8,128]{2,1,0:T(8,128)}, u32[]{:S(2)}) %copy-start.4) | copy-done | bytes 65560
  5.2 0.0 copy-start.5
  5.2 0.8 %copy-done.5 = f32[16,8,128]{2,1,0:T(8,128)S(1)} copy-done((f32[16,8,128]{2,1,0:T(8,128)S(1)}, f32[16,8,128]{2,1,0:T(8,128)}, u32[]{:S(2)}) %copy-start.5) | copy-done | bytes 65560
  6.0 32.2 %shard_map.85 = (f32[384,128]{1,0:T(8,128)S(1)}, f32[128,128]{1,0:T(8,128)S(1)}, f32[128,128]{1,0:T(8,128)S(1)}) custom-call(f32[384,128]{1,0:T(8,128)S(1)} %bitcast.9, f32[128,128]{1,0:T(8,128)S(1)} %bitcast.14, f32[384,128]{1,0:T(8,128)S(1)} %bitcast.10, f32[128,128]{1,0:T(8,128)S(1)} %bitcast.15, f32[384,128]{1,0:T(8,128)S(1)} %bitcast.11, ...), custom_call_target="tpu_custom_call" | custom-call | tf_op jit(solution)/shard_map/pallas_call | solution.py:473
  38.2 0.7 %copy.12 = f32[3,16,8,128]{3,2,1,0:T(8,128)} copy(f32[3,16,8,128]{3,2,1,0:T(8,128)S(1)} %bitcast.13) | data formatting | bytes 393216
  38.9 0.6 %copy.13 = f32[16,8,128]{2,1,0:T(8,128)} copy(f32[16,8,128]{2,1,0:T(8,128)S(1)} %bitcast.17) | data formatting | bytes 131072
  39.5 0.6 %copy.14 = f32[16,8,128]{2,1,0:T(8,128)} copy(f32[16,8,128]{2,1,0:T(8,128)S(1)} %bitcast.16) | data formatting | bytes 131072
Async XLA Ops:
  0.6 0.9 %copy-start = (f32[3,16,8,128]{3,2,1,0:T(8,128)S(1)}, f32[3,16,8,128]{3,2,1,0:T(8,128)}, u32[]{:S(2)}) copy-start(f32[3,16,8,128]{3,2,1,0:T(8,128)} %param.6) | copy-start | bytes 589828
  1.6 0.9 %copy-start.1 = (f32[3,16,8,128]{3,2,1,0:T(8,128)S(1)}, f32[3,16,8,128]{3,2,1,0:T(8,128)}, u32[]{:S(2)}) copy-start(f32[3,16,8,128]{3,2,1,0:T(8,128)} %param.8) | copy-start | bytes 589828
  2.5 0.9 %copy-start.2 = (f32[3,16,8,128]{3,2,1,0:T(8,128)S(1)}, f32[3,16,8,128]{3,2,1,0:T(8,128)}, u32[]{:S(2)}) copy-start(f32[3,16,8,128]{3,2,1,0:T(8,128)} %param.10) | copy-start | bytes 589828
  3.4 0.9 %copy-start.3 = (f32[3,16,8,128]{3,2,1,0:T(8,128)S(1)}, f32[3,16,8,128]{3,2,1,0:T(8,128)}, u32[]{:S(2)}) copy-start(f32[3,16,8,128]{3,2,1,0:T(8,128)} %param.11) | copy-start | bytes 589828
  4.3 0.8 %copy-start.4 = (f32[16,8,128]{2,1,0:T(8,128)S(1)}, f32[16,8,128]{2,1,0:T(8,128)}, u32[]{:S(2)}) copy-start(f32[16,8,128]{2,1,0:T(8,128)} %param.7) | copy-start | bytes 196612
  5.2 0.8 %copy-start.5 = (f32[16,8,128]{2,1,0:T(8,128)S(1)}, f32[16,8,128]{2,1,0:T(8,128)}, u32[]{:S(2)}) copy-start(f32[16,8,128]{2,1,0:T(8,128)} %param.9) | copy-start | bytes 196612

commit v2 on v1

--- a/solution.py
+++ b/solution.py
@@ -79,17 +79,28 @@
     def zm(a):
         return jnp.where(ground, 0.0, pltpu.roll(a, 1, 0))
 
+    def grouped(lo, hi, size, body):
+        count = (hi - lo) // size
+        if count == 1:
+            body(lo)
+            return
+
+        def step(n, _):
+            body(lo + n * size)
+            return 0
+        lax.fori_loop(0, count, step, 0)
+
     def load_half(b):
-        def one(j, _):
-            for f in range(b * HALF, b * HALF + HALF):
-                value = cells[pl.ds(ORDER[f] * plane + j, nz, stride=ny_dev), :]
-                if f == CY:
-                    value = jnp.where(gy * ny_dev + j == 0, 0.0, value)
-                if f == CZ:
-                    value = jnp.where(level == 0, 0.0, value)
-                rows[3 + j, f] = value
-            return 0
-        lax.fori_loop(0, ny_dev, one, 0)
+        def some(j0):
+            for j in (j0, j0 + 1):
+                for f in range(b * HALF, b * HALF + HALF):
+                    value = cells[pl.ds(ORDER[f] * plane + j, nz, stride=ny_dev), :]
+                    if f == CY:
+                        value = jnp.where(gy * ny_dev + j == 0, 0.0, value)
+                    if f == CZ:
+                        value = jnp.where(level == 0, 0.0, value)
+                    rows[3 + j, f] = value
+        grouped(0, ny_dev, 2, some)
 
     def pack_half(b):
         def one(t, _):
@@ -204,90 +215,97 @@
     def wide(r, f):
         return jnp.concatenate([rows[r, f], edges[r, f]], axis=1)
 
-    def upwind(fields, lo, hi):
-        def one(r, _):
-            cx, cy, cy_up, cz = wide(r, CX), wide(r, CY), wide(r + 1, CY), wide(r, CZ)
-            inv = 1.0 / wide(r, RHO)
-            cx_p, cx_n = jnp.maximum(cx, 0.0), jnp.minimum(cx, 0.0)
-            cy_p, cy_n = jnp.maximum(cy, 0.0), jnp.minimum(cy, 0.0)
-            cu_p, cu_n = jnp.maximum(cy_up, 0.0), jnp.minimum(cy_up, 0.0)
-            cz_p, cz_n = jnp.maximum(cz, 0.0), jnp.minimum(cz, 0.0)
-            for n, f in fields:
-                here = wide(r, f)
-                fx = cx_p * xm(here) + cx_n * here
-                fz = cz_p * zm(here) + cz_n * here
-                fy = cy_p * wide(r - 1, f) + cy_n * here
-                fu = cu_p * here + cu_n * wide(r + 1, f)
-                total = xp(fx) - fx + fu - fy + zp(fz) - fz
-                first[r, n] = here - total * inv
-            return 0
-        lax.fori_loop(lo, hi, one, 0)
-
-    def antidiffuse(fields, lo, hi):
-        def one(r, _):
-            cx, cy, cy_up, cz = wide(r, CX), wide(r, CY), wide(r + 1, CY), wide(r, CZ)
-            rho = wide(r, RHO)
-            inv = 1.0 / rho
-
-            def face(c, a, b):
-                return 0.5 * jnp.abs(c) - c * c / (a + b)
-
-            kx = face(cx, xm(rho), rho)
-            ky = face(cy, wide(r - 1, RHO), rho)
-            ku = face(cy_up, rho, wide(r + 1, RHO))
-            kz = face(cz, zm(rho), rho)
-            for n in fields:
-                here = first[r, n]
-                ax = kx * (here - xm(here))
-                az = kz * (here - zm(here))
-                ay = ky * (here - first[r - 1, n])
-                au = ku * (first[r + 1, n] - here)
-                total = xp(ax) - ax + au - ay + zp(az) - az
-                second[r, n] = here - total * inv
-            return 0
-        lax.fori_loop(lo, hi, one, 0)
+    def upwind(fields, lo, hi, size):
+        def some(r0):
+            span = range(size)
+            cys = [wide(r0 + i, CY) for i in range(size + 1)]
+            cys = [(jnp.maximum(c, 0.0), jnp.minimum(c, 0.0)) for c in cys]
+            psi = {f: [wide(r0 + i - 1, f) for i in range(size + 2)] for _, f in fields}
+            for i in span:
+                r = r0 + i
+                cx, cz = wide(r, CX), wide(r, CZ)
+                inv = 1.0 / wide(r, RHO)
+                cx_p, cx_n = jnp.maximum(cx, 0.0), jnp.minimum(cx, 0.0)
+                cz_p, cz_n = jnp.maximum(cz, 0.0), jnp.minimum(cz, 0.0)
+                for n, f in fields:
+                    below, here, above = psi[f][i:i + 3]
+                    fx = cx_p * xm(here) + cx_n * here
+                    fz = cz_p * zm(here) + cz_n * here
+                    fy = cys[i][0] * below + cys[i][1] * here
+                    fu = cys[i + 1][0] * here + cys[i + 1][1] * above
+                    total = xp(fx) - fx + fu - fy + zp(fz) - fz
+                    first[r, n] = here - total * inv
+        grouped(lo, hi, size, some)
+
+    def face(c, a, b):
+        return 0.5 * jnp.abs(c) - c * c / (a + b)
+
+    def antidiffuse(fields, lo, hi, size):
+        def some(r0):
+            rhos = [wide(r0 + i - 1, RHO) for i in range(size + 2)]
+            kys = [face(wide(r0 + i, CY), rhos[i], rhos[i + 1]) for i in range(size + 1)]
+            for i in range(size):
+                r = r0 + i
+                rho = rhos[i + 1]
+                inv = 1.0 / rho
+                kx = face(wide(r, CX), xm(rho), rho)
+                kz = face(wide(r, CZ), zm(rho), rho)
+                for n in fields:
+                    here = first[r, n]
+                    ax = kx * (here - xm(here))
+                    az = kz * (here - zm(here))
+                    ay = kys[i] * (here - first[r - 1, n])
+                    au = kys[i + 1] * (first[r + 1, n] - here)
+                    total = xp(ax) - ax + au - ay + zp(az) - az
+                    second[r, n] = here - total * inv
+        grouped(lo, hi, size, some)
 
     wait_recv(half_a)
     unpack_half(0)
-    upwind(((0, U), (1, V), (2, W)), 1, 13)
-    antidiffuse((0, 1, 2), 2, 12)
-
-    def make_rhs(j, acc):
+    upwind(((0, U), (1, V), (2, W)), 1, 13, 3)
+    antidiffuse((0, 1, 2), 2, 12, 2)
+
+    acc = jnp.zeros((nz, 128), jnp.float32)
+    for j in range(ny_dev):
         r = 3 + j
         u, w = second[r, 0], second[r, 2]
         value = (0.5 * (xp(u) - xm(u)) + 0.5 * (second[r + 1, 1] - second[r - 1, 1])
                  + 0.5 * (zp(w) - zm(w)))[:, :128]
         rhs_rows[r] = value
-        return jnp.where(slot == j, pltpu.roll(value, 8 * j + 4, 1), acc)
-
-    rhs_packed[...] = lax.fori_loop(0, ny_dev, make_rhs, jnp.zeros((nz, 128), jnp.float32))
+        acc = jnp.where(slot == j, pltpu.roll(value, 8 * j + 4, 1), acc)
+    rhs_packed[...] = acc
     start(half_r)
 
     wait_recv(half_b)
     unpack_half(1)
 
-    def make_coef(r, _):
-        a11, a22, a33 = wide(r, A11), wide(r, A22), wide(r, A33)
-        at = gy * ny_dev + r - 3
-        wxl = 0.5 * (xm(a11) + a11)
-        wx = xp(wxl)
-        wyl = jnp.where((at > 0) & (at < ny * ny_dev), 0.5 * (wide(r - 1, A22) + a22), 0.0)
-        wy = jnp.where((at > -1) & (at < ny * ny_dev - 1), 0.5 * (a22 + wide(r + 1, A22)), 0.0)
-        wzl = jnp.where(ground, 0.0, 0.5 * (zm(a33) + a33))
-        wz = zp(wzl)
-        coef[r, 0] = wx
-        coef[r, 1] = wxl
-        coef[r, 2] = wy
-        coef[r, 3] = wyl
-        coef[r, 4] = wz
-        coef[r, 5] = wzl
-        coef[r, 6] = (SHIFT - HELM) - (wx + wxl + wy + wyl + wz + wzl)
-        coef[r, 7] = 0.25 * wide(r, A12)
-        coef[r, 8] = 0.25 * wide(r, A13)
-        coef[r, 9] = 0.25 * wide(r, A23)
-        return 0
-
-    lax.fori_loop(1, 13, make_coef, 0)
+    def make_coef(r0):
+        size = 4
+        a22s = [wide(r0 + i - 1, A22) for i in range(size + 2)]
+        wys = []
+        for i in range(size + 1):
+            at = gy * ny_dev + r0 + i - 3
+            wys.append(jnp.where((at > 0) & (at < ny * ny_dev), 0.5 * (a22s[i] + a22s[i + 1]), 0.0))
+        for i in range(size):
+            r = r0 + i
+            a11, a33 = wide(r, A11), wide(r, A33)
+            wxl = 0.5 * (xm(a11) + a11)
+            wx = xp(wxl)
+            wyl, wy = wys[i], wys[i + 1]
+            wzl = jnp.where(ground, 0.0, 0.5 * (zm(a33) + a33))
+            wz = zp(wzl)
+            coef[r, 0] = wx
+            coef[r, 1] = wxl
+            coef[r, 2] = wy
+            coef[r, 3] = wyl
+            coef[r, 4] = wz
+            coef[r, 5] = wzl
+            coef[r, 6] = (SHIFT - HELM) - (wx + wxl + wy + wyl + wz + wzl)
+            coef[r, 7] = 0.25 * wide(r, A12)
+            coef[r, 8] = 0.25 * wide(r, A13)
+            coef[r, 9] = 0.25 * wide(r, A23)
+
+    grouped(1, 13, 4, make_coef)
 
     wait_recv(half_r)
 
@@ -314,33 +332,43 @@
     halo_rhs(0, (5, 6, 7), 0, gy > 0)
     halo_rhs(1, (0, 1, 2), 11, gy < ny - 1)
 
-    def operate(n, r):
-        p, up, down = kry[n, r], kry[n, r + 1], kry[n, r - 1]
-        right, left = xp(p), xm(p)
-        dx = right - left
-        dy = up - down
-        return (coef[r, 0] * right + coef[r, 1] * left + coef[r, 2] * up + coef[r, 3] * down
+    def operate(n, r0, size):
+        ps = [kry[n, r0 + i - 1] for i in range(size + 2)]
+        sides = [(xp(p), xm(p)) for p in ps]
+        dxs = [right - left for right, left in sides]
+        out = []
+        for i in range(size):
+            r = r0 + i
+            down, p, up = ps[i:i + 3]
+            right, left = sides[i + 1]
+            dx, dy = dxs[i + 1], up - down
+            out.append(
+                coef[r, 0] * right + coef[r, 1] * left + coef[r, 2] * up + coef[r, 3] * down
                 + coef[r, 4] * zp(p) + coef[r, 5] * zm(p) + coef[r, 6] * p
-                + coef[r, 7] * ((xp(up) - xm(up)) - (xp(down) - xm(down)))
+                + coef[r, 7] * (dxs[i + 2] - dxs[i])
                 + coef[r, 8] * (zp(dx) - zm(dx)) + coef[r, 9] * (zp(dy) - zm(dy)))
-
-    for n in range(2):
-        def lift(r, _, n=n):
-            kry[n + 1, r] = operate(n, r)
-            return 0
-        lax.fori_loop(1 + n, 13 - n, lift, 0)
+        return out
+
+    for n, size in ((0, 4), (1, 5)):
+        def lift(r0, n=n, size=size):
+            for i, value in enumerate(operate(n, r0, size)):
+                kry[n + 1, r0 + i] = value
+        grouped(1 + n, 13 - n, size, lift)
 
     pairs = [(a, b) for a in range(ITERS + 1) for b in range(a, ITERS + 1)]
 
-    def gram(r, acc):
-        vecs = [kry[n, r][:, :128] for n in range(ITERS)] + [operate(ITERS - 1, r)[:, :128]]
-        out = []
-        for (a, b), s in zip(pairs, acc):
-            prod = vecs[a] * vecs[b]
-            out.append(s + (prod[:8] + prod[8:]))
-        return tuple(out)
-
-    sums = lax.fori_loop(3, 3 + ny_dev, gram, tuple(jnp.zeros((8, 128), jnp.float32) for _ in pairs))
+    def gram(step, acc):
+        r0 = 3 + 4 * step
+        tops = operate(ITERS - 1, r0, 4)
+        acc = list(acc)
+        for i in range(4):
+            vecs = [kry[n, r0 + i][:, :128] for n in range(ITERS)] + [tops[i][:, :128]]
+            for n, (a, b) in enumerate(pairs):
+                prod = vecs[a] * vecs[b]
+                acc[n] = acc[n] + (prod[:8] + prod[8:])
+        return tuple(acc)
+
+    sums = lax.fori_loop(0, ny_dev // 4, gram, tuple(jnp.zeros((8, 128), jnp.float32) for _ in pairs))
     spot = lax.broadcasted_iota(jnp.int32, (16, 128), 0)
     tile = jnp.zeros((16, 128), jnp.float32)
     for n, s in enumerate(sums):
@@ -361,7 +389,7 @@
 
     for d in range(1, nx):
         x_copy(d).start()
-    upwind(((3, TH),), 2, 12)
+    upwind(((3, TH),), 2, 12, 5)
     for d in range(1, nx):
         x_copy(d).wait_recv()
     tile = part[...]
@@ -370,16 +398,13 @@
     sum_x[...] = tile
     for d in range(1, ny):
         y_copy(d).start()
-    antidiffuse((3,), 3, 11)
+    antidiffuse((3,), 3, 11, 4)
 
     def store(ref, base, j, value):
         ref[pl.ds(base + j, nz, stride=ny_dev), :] = value
 
-    def put_theta(j, _):
+    for j in range(ny_dev):
         store(th_out, 0, j, second[3 + j, 3][:, :128])
-        return 0
-
-    lax.fori_loop(0, ny_dev, put_theta, 0)
     for d in range(1, ny):
         y_copy(d).wait_recv()
     tile = sum_x[...]
@@ -436,17 +461,19 @@
     def pressure(r):
         return c0 * kry[0, r] + c1 * kry[1, r] + c2 * kry[2, r]
 
-    def finish(j, carry):
-        down, here = carry
-        r = 3 + j
-        up = pressure(r + 1)
-        store(p_out, 0, j, here[:, :128])
-        store(mom_out, 0, j, (second[r, 0] - 0.5 * (xp(here) - xm(here)))[:, :128])
-        store(mom_out, plane, j, (second[r, 1] - 0.5 * (up - down))[:, :128])
-        store(mom_out, 2 * plane, j, (second[r, 2] - 0.5 * (zp(here) - zm(here)))[:, :128])
-        return here, up
-
-    lax.fori_loop(0, ny_dev, finish, (pressure(2), pressure(3)))
+    def finish(j0):
+        size = 4
+        ps = [pressure(3 + j0 + i - 1) for i in range(size + 2)]
+        for i in range(size):
+            j = j0 + i
+            r = 3 + j
+            down, here, up = ps[i:i + 3]
+            store(p_out, 0, j, here[:, :128])
+            store(mom_out, 0, j, (second[r, 0] - 0.5 * (xp(here) - xm(here)))[:, :128])
+            store(mom_out, plane, j, (second[r, 1] - 0.5 * (up - down))[:, :128])
+            store(mom_out, 2 * plane, j, (second[r, 2] - 0.5 * (zp(here) - zm(here)))[:, :128])
+
+    grouped(0, ny_dev, 4, finish)
 
     wait_send(half_a)
     wait_send(half_b)
@@ -474,7 +501,7 @@
             functools.partial(kernel, nx, ny),
             out_shape=(shape((3 * plane, nx_dev), f32), shape((plane, nx_dev), f32),
                        shape((plane, nx_dev), f32)),
-            in_specs=[pl.BlockSpec(memory_space=pl.ANY)] * 6,
+            in_specs=[pl.BlockSpec(memory_space=pltpu.HBM)] * 6,
             out_specs=[pl.BlockSpec(memory_space=pltpu.VMEM)] * 3,
             scratch_shapes=[
                 vmem((14 * plane, nx_dev), f32),
@@ -501,7 +528,7 @@
                 pltpu.SemaphoreType.DMA((n_sem,)),
             ],
             compiler_params=pltpu.CompilerParams(
-                collective_id=0, has_side_effects=True, vmem_limit_bytes=40 * 1024 * 1024),
+                collective_id=0, has_side_effects=True, vmem_limit_bytes=60 * 1024 * 1024),
         )(*flat)
         return mom.reshape(momenta.shape), th.reshape(theta.shape), press.reshape(theta.shape)
 

time: 40.5 us -> 31.6 us (0.78)
  Pallas kernels: 32.2 us -> 27.6 us
  local copies, waits for them, and re-layouts: 7.31 us -> 3.14 us
    pallas_call x1, Pallas kernels: 32.2 us -> 27.6 us  [local(): pl.pallas_call(functools.partial(kernel, nx, ny), out_shape=(shape((3 * p...]
    unnamed x15 -> x7, local copies, waits for them, and re-layouts: 7.31 us -> 3.14 us
where the time goes in v2:
time: 31.6 us; the launch traced here: 31.4 us
  Pallas kernels  27.6 us (87%)
  local copies, waits for them, and re-layouts  3.14 us (10%)
  between operations  0.65 us (2%)
    pallas_call x1, Pallas kernels, local(): pl.pallas_call(functools.partial(kernel, nx, ny), out_shape=(shape((3 * p...  27.6 us
    unnamed x7, local copies, waits for them, and re-layouts  3.14 us

profile of v2, /device:TPU:0, one launch (start us, length us, event | category | flops | bytes accessed | tf_op | source)
XLA Modules:
  0.0 31.4 jit_solution(15594199653252153703)
XLA Ops:
  0.6 27.6 %shard_map.85 = (f32[384,128]{1,0:T(8,128)}, f32[128,128]{1,0:T(8,128)}, f32[128,128]{1,0:T(8,128)}) custom-call(f32[384,128]{1,0:T(8,128)} %bitcast.9, f32[128,128]{1,0:T(8,128)} %bitcast.14, f32[384,128]{1,0:T(8,128)} %bitcast.10, f32[128,128]{1,0:T(8,128)} %bitcast.15, f32[384,128]{1,0:T(8,128)} %bitcast.11, f32[384,128]{1,0:T(8,128)} %bitcast.12), custom_call_target="tpu_custom_call" | custom-call | tf_op jit(solution)/shard_map/pallas_call | solution.py:500
  28.3 0.0 copy-start.1
  28.3 1.6 %copy.12 = f32[3,16,8,128]{3,2,1,0:T(8,128)} copy(f32[3,16,8,128]{3,2,1,0:T(8,128)} %bitcast.13) | data formatting | bytes 393216
  29.9 0.0 copy-done.1
  29.9 0.0 copy-start
  29.9 0.6 %copy.13 = f32[16,8,128]{2,1,0:T(8,128)} copy(f32[16,8,128]{2,1,0:T(8,128)S(1)} %bitcast.17) | data formatting | bytes 131072
  30.6 0.2 copy-done
  30.8 0.6 %copy.14 = f32[16,8,128]{2,1,0:T(8,128)} copy(f32[16,8,128]{2,1,0:T(8,128)S(1)} %bitcast.16) | data formatting | bytes 131072
Async XLA Ops:
  28.3 1.7 %copy-start.1 = (f32[128,128]{1,0:T(8,128)S(1)}, f32[128,128]{1,0:T(8,128)}, u32[]{:S(2)}) copy-start(f32[128,128]{1,0:T(8,128)} %get-tuple-element.7) | copy-start | bytes 196612
  29.9 0.9 %copy-start = (f32[128,128]{1,0:T(8,128)S(1)}, f32[128,128]{1,0:T(8,128)}, u32[]{:S(2)}) copy-start(f32[128,128]{1,0:T(8,128)} %get-tuple-element.8) | copy-start | bytes 196612

commit v3 on v2

--- a/solution.py
+++ b/solution.py
@@ -20,7 +20,7 @@
 
 def kernel(nx, ny, mom, theta, cour, dens, diag, cross, mom_out, th_out, p_out,
            cells, rows, edges, packed, beside, corner, first, second, coef,
-           kry, rhs_rows, rhs_edges, rhs_packed, rhs_beside, rhs_corner,
+           kry, rhs_rows, rhs_packed, rhs_beside, rhs_corner,
            part, part_x, sum_x, part_y, in_sem, send_sem, recv_sem):
     gx = lax.axis_index("gx")
     gy = lax.axis_index("gy")
@@ -54,7 +54,6 @@
             rows[i, RHO] = jnp.ones(rows.shape[2:], jnp.float32)
             edges[i, RHO] = jnp.ones(rows.shape[2:], jnp.float32)
         rhs_rows[lo:lo + 3] = jnp.zeros((3,) + rhs_rows.shape[1:], jnp.float32)
-        rhs_edges[lo:lo + 3] = jnp.zeros((3,) + rhs_edges.shape[1:], jnp.float32)
 
     pl.when(gy == 0)(lambda: clear(0))
     pl.when(gy == ny - 1)(lambda: clear(11))
@@ -79,14 +78,15 @@
     def zm(a):
         return jnp.where(ground, 0.0, pltpu.roll(a, 1, 0))
 
-    def grouped(lo, hi, size, body):
-        count = (hi - lo) // size
+    def grouped(lo, hi, size, body, stride=None):
+        stride = size if stride is None else stride
+        count = (hi - lo) // stride
         if count == 1:
             body(lo)
             return
 
         def step(n, _):
-            body(lo + n * size)
+            body(lo + n * stride)
             return 0
         lax.fori_loop(0, count, step, 0)
 
@@ -110,34 +110,37 @@
                     p = 64 * side + 8 * fi
                     moved = pltpu.roll(rows[3 + 2 * t + side, b * HALF + fi], (p + 4) % 128, 1)
                     acc = jnp.where(slot == p // 8, moved, acc)
+            for fi in range(THIRD[b]):
+                p = 56 + 64 * fi
+                moved = pltpu.roll(rows[5 + 3 * (t // 2), b * HALF + fi], (p + 4) % 128, 1)
+                acc = jnp.where(slot == p // 8, moved, acc)
             packed[b, t] = acc
             return 0
         lax.fori_loop(0, ny_dev // 2, one, 0)
 
-    def unpack_half(b):
-        def spread(tile, side, row, count):
-            for fi in range(count):
-                p = 64 * side + 8 * fi
-                edges[row, b * HALF + fi] = pltpu.roll(tile, (128 - (p + 4)) % 128, 1)
-
+    def spread(b, tile, side, row):
+        for fi in range(HALF):
+            p = 64 * side + 8 * fi
+            edges[row, b * HALF + fi] = pltpu.roll(tile, (128 - (p + 4)) % 128, 1)
+
+    def unpack_own(b):
         def one(t, _):
             tile = jnp.where(from_left, beside[b, 0, t], beside[b, 1, t])
             for side in range(2):
-                spread(tile, side, 3 + 2 * t + side, HALF)
+                spread(b, tile, side, 3 + 2 * t + side)
             return 0
         lax.fori_loop(0, ny_dev // 2, one, 0)
 
-        @pl.when(gy > 0)
-        def _():
-            for j in (5, 6, 7):
-                tile = jnp.where(from_left, corner[b, 0, 0, j // 2 - 2], corner[b, 0, 1, j // 2 - 2])
-                spread(tile, j % 2, j - 5, THIRD[b] if j == 5 else HALF)
-
-        @pl.when(gy < ny - 1)
-        def _():
-            for j in (0, 1, 2):
-                tile = jnp.where(from_left, corner[b, 1, 0, j // 2], corner[b, 1, 1, j // 2])
-                spread(tile, j % 2, 11 + j, THIRD[b] if j == 2 else HALF)
+    def unpack_halo(b):
+        def one(side, near, third):
+            tile = jnp.where(from_left, corner[b, side, 0], corner[b, side, 1])
+            spread(b, tile, 0, near)
+            spread(b, tile, 1, near + 1)
+            for fi in range(THIRD[b]):
+                edges[third, b * HALF + fi] = pltpu.roll(tile, (128 - (60 + 64 * fi)) % 128, 1)
+
+        pl.when(gy > 0)(lambda: one(0, 1, 0))
+        pl.when(gy < ny - 1)(lambda: one(1, 11, 13))
 
     def remote(src, dst, k, dx, dy):
         return pltpu.make_async_remote_copy(
@@ -150,8 +153,8 @@
             by[dy].append((src, dst, base + n, dx, dy))
         return by
 
-    def each(by, action, sign):
-        for dy in (1, -1, 0):
+    def each(by, action, sign, order=(0, 1, -1)):
+        for dy in order:
             def run(dy=dy):
                 for item in by[dy]:
                     action(remote(*item))
@@ -165,8 +168,11 @@
     def start(by):
         each(by, lambda c: c.start(), 1)
 
-    def wait_recv(by):
-        each(by, lambda c: c.wait_recv(), -1)
+    def wait_beside(by):
+        each(by, lambda c: c.wait_recv(), -1, (0,))
+
+    def wait_halo(by):
+        each(by, lambda c: c.wait_recv(), -1, (1, -1))
 
     def wait_send(by):
         each(by, lambda c: c.wait_send(), 1)
@@ -181,10 +187,10 @@
             (0, -1, rows.at[pl.ds(5, 1), ft], rows.at[pl.ds(13, 1), ft]),
             (1, 0, packed.at[b], beside.at[b, 0]),
             (-1, 0, packed.at[b], beside.at[b, 1]),
-            (1, 1, packed.at[b, pl.ds(2, 2)], corner.at[b, 0, 0]),
-            (-1, 1, packed.at[b, pl.ds(2, 2)], corner.at[b, 0, 1]),
-            (1, -1, packed.at[b, pl.ds(0, 2)], corner.at[b, 1, 0]),
-            (-1, -1, packed.at[b, pl.ds(0, 2)], corner.at[b, 1, 1]),
+            (1, 1, packed.at[b, 3], corner.at[b, 0, 0]),
+            (-1, 1, packed.at[b, 3], corner.at[b, 0, 1]),
+            (1, -1, packed.at[b, 0], corner.at[b, 1, 0]),
+            (-1, -1, packed.at[b, 0], corner.at[b, 1, 1]),
         ]
 
     half_a = group(half_entries(0), 0)
@@ -215,7 +221,7 @@
     def wide(r, f):
         return jnp.concatenate([rows[r, f], edges[r, f]], axis=1)
 
-    def upwind(fields, lo, hi, size):
+    def upwind(fields, lo, hi, size, stride=None):
         def some(r0):
             span = range(size)
             cys = [wide(r0 + i, CY) for i in range(size + 1)]
@@ -235,12 +241,12 @@
                     fu = cys[i + 1][0] * here + cys[i + 1][1] * above
                     total = xp(fx) - fx + fu - fy + zp(fz) - fz
                     first[r, n] = here - total * inv
-        grouped(lo, hi, size, some)
+        grouped(lo, hi, size, some, stride)
 
     def face(c, a, b):
         return 0.5 * jnp.abs(c) - c * c / (a + b)
 
-    def antidiffuse(fields, lo, hi, size):
+    def antidiffuse(fields, lo, hi, size, stride=None):
         def some(r0):
             rhos = [wide(r0 + i - 1, RHO) for i in range(size + 2)]
             kys = [face(wide(r0 + i, CY), rhos[i], rhos[i + 1]) for i in range(size + 1)]
@@ -258,12 +264,17 @@
                     au = kys[i + 1] * (first[r + 1, n] - here)
                     total = xp(ax) - ax + au - ay + zp(az) - az
                     second[r, n] = here - total * inv
-        grouped(lo, hi, size, some)
-
-    wait_recv(half_a)
-    unpack_half(0)
-    upwind(((0, U), (1, V), (2, W)), 1, 13, 3)
-    antidiffuse((0, 1, 2), 2, 12, 2)
+        grouped(lo, hi, size, some, stride)
+
+    wind = ((0, U), (1, V), (2, W))
+    wait_beside(half_a)
+    unpack_own(0)
+    upwind(wind, 4, 10, 3)
+    antidiffuse((0, 1, 2), 5, 9, 2)
+    wait_halo(half_a)
+    unpack_halo(0)
+    upwind(wind, 1, 19, 3, 9)
+    antidiffuse((0, 1, 2), 2, 16, 3, 7)
 
     acc = jnp.zeros((nz, 128), jnp.float32)
     for j in range(ny_dev):
@@ -276,8 +287,10 @@
     rhs_packed[...] = acc
     start(half_r)
 
-    wait_recv(half_b)
-    unpack_half(1)
+    wait_beside(half_b)
+    unpack_own(1)
+    wait_halo(half_b)
+    unpack_halo(1)
 
     def make_coef(r0):
         size = 4
@@ -307,15 +320,9 @@
 
     grouped(1, 13, 4, make_coef)
 
-    wait_recv(half_r)
-
     def spread_rhs(j, tile, row):
         edge = pltpu.roll(tile, 128 - (8 * j + 4), 1)
         kry[0, row] = jnp.concatenate([rhs_rows[row], edge], axis=1)
-
-    tile = jnp.where(from_left, rhs_beside[0], rhs_beside[1])
-    for j in range(ny_dev):
-        spread_rhs(j, tile, 3 + j)
 
     def halo_rhs(side, js, lo, inside):
         @pl.when(inside)
@@ -328,9 +335,6 @@
         def _():
             for n in range(3):
                 kry[0, lo + n] = jnp.zeros((nz, 256), jnp.float32)
-
-    halo_rhs(0, (5, 6, 7), 0, gy > 0)
-    halo_rhs(1, (0, 1, 2), 11, gy < ny - 1)
 
     def operate(n, r0, size):
         ps = [kry[n, r0 + i - 1] for i in range(size + 2)]
@@ -349,26 +353,37 @@
                 + coef[r, 8] * (zp(dx) - zm(dx)) + coef[r, 9] * (zp(dy) - zm(dy)))
         return out
 
-    for n, size in ((0, 4), (1, 5)):
-        def lift(r0, n=n, size=size):
+    def lift(n, lo, hi, size, stride=None):
+        def some(r0):
             for i, value in enumerate(operate(n, r0, size)):
                 kry[n + 1, r0 + i] = value
-        grouped(1 + n, 13 - n, size, lift)
+        grouped(lo, hi, size, some, stride)
 
     pairs = [(a, b) for a in range(ITERS + 1) for b in range(a, ITERS + 1)]
 
-    def gram(step, acc):
-        r0 = 3 + 4 * step
-        tops = operate(ITERS - 1, r0, 4)
+    def gram(acc, r0, size):
+        tops = operate(ITERS - 1, r0, size)
         acc = list(acc)
-        for i in range(4):
+        for i in range(size):
             vecs = [kry[n, r0 + i][:, :128] for n in range(ITERS)] + [tops[i][:, :128]]
             for n, (a, b) in enumerate(pairs):
                 prod = vecs[a] * vecs[b]
                 acc[n] = acc[n] + (prod[:8] + prod[8:])
         return tuple(acc)
 
-    sums = lax.fori_loop(0, ny_dev // 4, gram, tuple(jnp.zeros((8, 128), jnp.float32) for _ in pairs))
+    wait_beside(half_r)
+    tile = jnp.where(from_left, rhs_beside[0], rhs_beside[1])
+    for j in range(ny_dev):
+        spread_rhs(j, tile, 3 + j)
+    lift(0, 4, 10, 3)
+    lift(1, 5, 9, 4)
+    sums = gram(tuple(jnp.zeros((8, 128), jnp.float32) for _ in pairs), 6, 2)
+    wait_halo(half_r)
+    halo_rhs(0, (5, 6, 7), 0, gy > 0)
+    halo_rhs(1, (0, 1, 2), 11, gy < ny - 1)
+    lift(0, 1, 19, 3, 9)
+    lift(1, 2, 16, 3, 7)
+    sums = lax.fori_loop(0, 2, lambda n, acc: gram(acc, 3 + 5 * n, 3), sums)
     spot = lax.broadcasted_iota(jnp.int32, (16, 128), 0)
     tile = jnp.zeros((16, 128), jnp.float32)
     for n, s in enumerate(sums):
@@ -509,12 +524,11 @@
                 vmem((n_ext, 14, nz, nx_dev), f32),
                 vmem((2, 4, nz, nx_dev), f32),
                 vmem((2, 2, 4, nz, nx_dev), f32),
-                vmem((2, 2, 2, 2, nz, nx_dev), f32),
+                vmem((2, 2, 2, nz, nx_dev), f32),
                 vmem((n_ext, 4, nz, 2 * nx_dev), f32),
                 vmem((n_ext, 4, nz, 2 * nx_dev), f32),
                 vmem((n_ext, 10, nz, 2 * nx_dev), f32),
                 vmem((3, n_ext, nz, 2 * nx_dev), f32),
-                vmem((n_ext, nz, nx_dev), f32),
                 vmem((n_ext, nz, nx_dev), f32),
                 vmem((nz, nx_dev), f32),
                 vmem((2, nz, nx_dev), f32),

time: 31.6 us -> 29.8 us (0.943)
  Pallas kernels: 27.6 us -> 25.8 us
    pallas_call x1, Pallas kernels: 27.6 us -> 25.8 us  [local(): pl.pallas_call(functools.partial(kernel, nx, ny), out_shape=(shape((3 * p...]
where the time goes in v3:
time: 29.8 us; the launch traced here: 29.6 us
  Pallas kernels  25.8 us (87%)
  local copies, waits for them, and re-layouts  3.14 us (11%)
  between operations  0.65 us (2%)
    pallas_call x1, Pallas kernels, local(): pl.pallas_call(functools.partial(kernel, nx, ny), out_shape=(shape((3 * p...  25.8 us
    unnamed x7, local copies, waits for them, and re-layouts  3.14 us

profile of v3, /device:TPU:0, one launch (start us, length us, event | category | flops | bytes accessed | tf_op | source)
XLA Modules:
  0.0 29.6 jit_solution(13569976076577330835)
XLA Ops:
  0.6 25.8 %shard_map.85 = (f32[384,128]{1,0:T(8,128)}, f32[128,128]{1,0:T(8,128)}, f32[128,128]{1,0:T(8,128)}) custom-call(f32[384,128]{1,0:T(8,128)} %bitcast.9, f32[128,128]{1,0:T(8,128)} %bitcast.14, f32[384,128]{1,0:T(8,128)} %bitcast.10, f32[128,128]{1,0:T(8,128)} %bitcast.15, f32[384,128]{1,0:T(8,128)} %bitcast.11, f32[384,128]{1,0:T(8,128)} %bitcast.12), custom_call_target="tpu_custom_call" | custom-call | tf_op jit(solution)/shard_map/pallas_call | solution.py:515
  26.5 0.0 copy-start.1
  26.5 1.6 %copy.12 = f32[3,16,8,128]{3,2,1,0:T(8,128)} copy(f32[3,16,8,128]{3,2,1,0:T(8,128)} %bitcast.13) | data formatting | bytes 393216
  28.1 0.0 copy-done.1
  28.1 0.0 copy-start
  28.1 0.6 %copy.13 = f32[16,8,128]{2,1,0:T(8,128)} copy(f32[16,8,128]{2,1,0:T(8,128)S(1)} %bitcast.17) | data formatting | bytes 131072
  28.8 0.2 copy-done
  29.0 0.6 %copy.14 = f32[16,8,128]{2,1,0:T(8,128)} copy(f32[16,8,128]{2,1,0:T(8,128)S(1)} %bitcast.16) | data formatting | bytes 131072
Async XLA Ops:
  26.5 1.7 %copy-start.1 = (f32[128,128]{1,0:T(8,128)S(1)}, f32[128,128]{1,0:T(8,128)}, u32[]{:S(2)}) copy-start(f32[128,128]{1,0:T(8,128)} %get-tuple-element.7) | copy-start | bytes 196612
  28.1 0.9 %copy-start = (f32[128,128]{1,0:T(8,128)S(1)}, f32[128,128]{1,0:T(8,128)}, u32[]{:S(2)}) copy-start(f32[128,128]{1,0:T(8,128)} %get-tuple-element.8) | copy-start | bytes 196612

commit v4 on v3

--- a/solution.py
+++ b/solution.py
@@ -499,13 +499,22 @@
         y_copy(d).wait_send()
 
 
+def put_out(mom, th, press, mom_out, th_out, p_out, sem):
+    pairs = ((mom, mom_out), (th, th_out), (press, p_out))
+    copies = [pltpu.make_async_copy(a, b, sem.at[n]) for n, (a, b) in enumerate(pairs)]
+    for copy in copies:
+        copy.start()
+    for copy in copies:
+        copy.wait()
+
+
 def solution(mesh):
     nx, ny = mesh.shape["gx"], mesh.shape["gy"]
 
     def local(momenta, theta, courant, density, metric_diag, metric_cross):
         nz, ny_dev, nx_dev = density.shape
         args = (momenta, theta, courant, density, metric_diag, metric_cross)
-        flat = [a.reshape(-1, nx_dev) for a in args]
+        flat = [pltpu.with_memory_space_constraint(a.reshape(-1, nx_dev), pltpu.HBM) for a in args]
         plane = nz * ny_dev
         f32 = jnp.float32
         n_ext = ny_dev + 6
@@ -542,8 +551,15 @@
                 pltpu.SemaphoreType.DMA((n_sem,)),
             ],
             compiler_params=pltpu.CompilerParams(
-                collective_id=0, has_side_effects=True, vmem_limit_bytes=60 * 1024 * 1024),
+                collective_id=0, has_side_effects=True, vmem_limit_bytes=40 * 1024 * 1024),
         )(*flat)
+        mom, th, press = pl.pallas_call(
+            put_out,
+            out_shape=[shape(a.shape, f32) for a in (mom, th, press)],
+            in_specs=[pl.BlockSpec(memory_space=pl.ANY)] * 3,
+            out_specs=[pl.BlockSpec(memory_space=pltpu.HBM)] * 3,
+            scratch_shapes=[pltpu.SemaphoreType.DMA((3,))],
+        )(mom, th, press)
         return mom.reshape(momenta.shape), th.reshape(theta.shape), press.reshape(theta.shape)
 
     placed = (

time: 29.8 us -> 38.8 us (1.30)
  Pallas kernels: 25.8 us -> 36.1 us
  local copies, waits for them, and re-layouts: 3.14 us -> 1.9 us
    pallas_call x0 -> x1, Pallas kernels: none -> 11.1 us  [local(): pl.pallas_call(put_out, out_shape=[shape(a.shape, f32) for a in (mom, th,...]
    unnamed x7 -> x6, local copies, waits for them, and re-layouts: 3.14 us -> 1.9 us
    pallas_call x1, Pallas kernels: 25.8 us -> 25.1 us  [local(): pl.pallas_call(functools.partial(kernel, nx, ny), out_shape=(shape((3 * p...]
where the time goes in v4:
time: 38.8 us; the launch traced here: 38.7 us
  Pallas kernels  36.1 us (93%)
  local copies, waits for them, and re-layouts  1.9 us (5%)
  between operations  0.65 us (2%)
    pallas_call x1, Pallas kernels, local(): pl.pallas_call(functools.partial(kernel, nx, ny), out_shape=(shape((3 * p...  25.1 us
    pallas_call x1, Pallas kernels, local(): pl.pallas_call(put_out, out_shape=[shape(a.shape, f32) for a in (mom, th,...  11.1 us
    unnamed x6, local copies, waits for them, and re-layouts  1.9 us

profile of v4, /device:TPU:0, one launch (start us, length us, event | category | flops | bytes accessed | tf_op | source)
XLA Modules:
  0.0 38.7 jit_solution(1429437231539488207)
XLA Ops:
  0.6 25.1 %shard_map.85 = (f32[384,128]{1,0:T(8,128)S(1)}, f32[128,128]{1,0:T(8,128)S(1)}, f32[128,128]{1,0:T(8,128)S(1)}) custom-call(f32[384,128]{1,0:T(8,128)} %bitcast.9, f32[128,128]{1,0:T(8,128)} %bitcast.13, f32[384,128]{1,0:T(8,128)} %bitcast.10, f32[128,128]{1,0:T(8,128)} %bitcast.14, f32[384,128]{1,0:T(8,128)} %bitcast.11, f32[384,128]{1,0:T(8,128)} %bitcast.12), custom_call_target="tpu_custom_call" | custom-call | tf_op jit(solution)/shard_map/pallas_call | solution.py:524
  25.7 0.0 copy-start
  25.7 0.7 %copy-done = f32[384,128]{1,0:T(8,128)} copy-done((f32[384,128]{1,0:T(8,128)}, f32[384,128]{1,0:T(8,128)S(1)}, u32[]{:S(2)}) %copy-start) | copy-done | bytes 196632
  26.4 0.0 copy-start.1
  26.4 0.6 %copy-done.1 = f32[128,128]{1,0:T(8,128)} copy-done((f32[128,128]{1,0:T(8,128)}, f32[128,128]{1,0:T(8,128)S(1)}, u32[]{:S(2)}) %copy-start.1) | copy-done | bytes 65560
  27.0 0.0 copy-start.2
  27.0 0.6 %copy-done.2 = f32[128,128]{1,0:T(8,128)} copy-done((f32[128,128]{1,0:T(8,128)}, f32[128,128]{1,0:T(8,128)S(1)}, u32[]{:S(2)}) %copy-start.2) | copy-done | bytes 65560
  27.6 11.1 %shard_map.86 = (f32[384,128]{1,0:T(8,128)}, f32[128,128]{1,0:T(8,128)}, f32[128,128]{1,0:T(8,128)}) custom-call(f32[384,128]{1,0:T(8,128)} %copy-done, f32[128,128]{1,0:T(8,128)} %copy-done.1, f32[128,128]{1,0:T(8,128)} %copy-done.2), custom_call_target="tpu_custom_call" | custom-call | tf_op jit(solution)/shard_map/pallas_call | solution.py:556
Async XLA Ops:
  25.7 0.7 %copy-start = (f32[384,128]{1,0:T(8,128)}, f32[384,128]{1,0:T(8,128)S(1)}, u32[]{:S(2)}) copy-start(f32[384,128]{1,0:T(8,128)S(1)} %get-tuple-element.9.mom) | copy-start | bytes 589828
  26.4 0.6 %copy-start.1 = (f32[128,128]{1,0:T(8,128)}, f32[128,128]{1,0:T(8,128)S(1)}, u32[]{:S(2)}) copy-start(f32[128,128]{1,0:T(8,128)S(1)} %get-tuple-element.10.th) | copy-start | bytes 196612
  27.0 0.6 %copy-start.2 = (f32[128,128]{1,0:T(8,128)}, f32[128,128]{1,0:T(8,128)S(1)}, u32[]{:S(2)}) copy-start(f32[128,128]{1,0:T(8,128)S(1)} %get-tuple-element.11.press) | copy-start | bytes 196612

commit v5 on v3

--- a/solution.py
+++ b/solution.py
@@ -21,7 +21,7 @@
 def kernel(nx, ny, mom, theta, cour, dens, diag, cross, mom_out, th_out, p_out,
            cells, rows, edges, packed, beside, corner, first, second, coef,
            kry, rhs_rows, rhs_packed, rhs_beside, rhs_corner,
-           part, part_x, sum_x, part_y, in_sem, send_sem, recv_sem):
+           part, parts, in_sem, send_sem, recv_sem):
     gx = lax.axis_index("gx")
     gy = lax.axis_index("gy")
     nz = rows.shape[2]
@@ -32,11 +32,24 @@
         return {"gx": lax.rem(gx + dx + nx, nx), "gy": gy + dy}
 
     barrier = pltpu.get_barrier_semaphore()
-    peers = [(lax.rem(gx + d, nx), gy) for d in range(1, nx)]
-    peers += [(gx, lax.rem(gy + d, ny)) for d in range(1, ny)]
-    peers += [(lax.rem(gx + a, nx), lax.rem(gy + b, ny)) for a in (1, nx - 1) for b in (1, ny - 1)]
-    for a, b in peers:
-        pl.semaphore_signal(barrier, inc=1, device_id={"gx": a, "gy": b}, device_id_type=MESH)
+    count = nx * ny
+    me = gx * ny + gy
+
+    def peer(d):
+        other = lax.rem(me + d, count)
+        return {"gx": other // ny, "gy": lax.rem(other, ny)}
+
+    def every_peer(body):
+        if count <= 64:
+            for d in range(1, count):
+                body(d)
+        else:
+            def step(d, _):
+                body(d)
+                return 0
+            lax.fori_loop(1, count, step, 0)
+
+    every_peer(lambda d: pl.semaphore_signal(barrier, inc=1, device_id=peer(d), device_id_type=MESH))
 
     loads = []
     place = 0
@@ -210,7 +223,7 @@
         loads[n].wait()
     load_half(0)
     pack_half(0)
-    pl.semaphore_wait(barrier, len(peers))
+    pl.semaphore_wait(barrier, count - 1)
     start(half_a)
     for n in (1, 4, 5):
         loads[n].wait()
@@ -224,21 +237,21 @@
     def upwind(fields, lo, hi, size, stride=None):
         def some(r0):
             span = range(size)
-            cys = [wide(r0 + i, CY) for i in range(size + 1)]
-            cys = [(jnp.maximum(c, 0.0), jnp.minimum(c, 0.0)) for c in cys]
-            psi = {f: [wide(r0 + i - 1, f) for i in range(size + 2)] for _, f in fields}
             for i in span:
                 r = r0 + i
                 cx, cz = wide(r, CX), wide(r, CZ)
                 inv = 1.0 / wide(r, RHO)
                 cx_p, cx_n = jnp.maximum(cx, 0.0), jnp.minimum(cx, 0.0)
                 cz_p, cz_n = jnp.maximum(cz, 0.0), jnp.minimum(cz, 0.0)
+                cy, cu = wide(r, CY), wide(r + 1, CY)
+                cy_p, cy_n = jnp.maximum(cy, 0.0), jnp.minimum(cy, 0.0)
+                cu_p, cu_n = jnp.maximum(cu, 0.0), jnp.minimum(cu, 0.0)
                 for n, f in fields:
-                    below, here, above = psi[f][i:i + 3]
+                    here = wide(r, f)
                     fx = cx_p * xm(here) + cx_n * here
                     fz = cz_p * zm(here) + cz_n * here
-                    fy = cys[i][0] * below + cys[i][1] * here
-                    fu = cys[i + 1][0] * here + cys[i + 1][1] * above
+                    fy = cy_p * wide(r - 1, f) + cy_n * here
+                    fu = cu_p * here + cu_n * wide(r + 1, f)
                     total = xp(fx) - fx + fu - fy + zp(fz) - fz
                     first[r, n] = here - total * inv
         grouped(lo, hi, size, some, stride)
@@ -248,20 +261,20 @@
 
     def antidiffuse(fields, lo, hi, size, stride=None):
         def some(r0):
-            rhos = [wide(r0 + i - 1, RHO) for i in range(size + 2)]
-            kys = [face(wide(r0 + i, CY), rhos[i], rhos[i + 1]) for i in range(size + 1)]
+            ku = face(wide(r0, CY), wide(r0 - 1, RHO), wide(r0, RHO))
             for i in range(size):
                 r = r0 + i
-                rho = rhos[i + 1]
+                rho = wide(r, RHO)
                 inv = 1.0 / rho
+                ky, ku = ku, face(wide(r + 1, CY), rho, wide(r + 1, RHO))
                 kx = face(wide(r, CX), xm(rho), rho)
                 kz = face(wide(r, CZ), zm(rho), rho)
                 for n in fields:
                     here = first[r, n]
                     ax = kx * (here - xm(here))
                     az = kz * (here - zm(here))
-                    ay = kys[i] * (here - first[r - 1, n])
-                    au = kys[i + 1] * (first[r + 1, n] - here)
+                    ay = ky * (here - first[r - 1, n])
+                    au = ku * (first[r + 1, n] - here)
                     total = xp(ax) - ax + au - ay + zp(az) - az
                     second[r, n] = here - total * inv
         grouped(lo, hi, size, some, stride)
@@ -337,19 +350,25 @@
                 kry[0, lo + n] = jnp.zeros((nz, 256), jnp.float32)
 
     def operate(n, r0, size):
-        ps = [kry[n, r0 + i - 1] for i in range(size + 2)]
-        sides = [(xp(p), xm(p)) for p in ps]
-        dxs = [right - left for right, left in sides]
+        def sides(r):
+            p = kry[n, r]
+            right, left = xp(p), xm(p)
+            return right, left, right - left
+
+        here, above = sides(r0), sides(r0 + 1)
+        below_dx = sides(r0 - 1)[2]
         out = []
         for i in range(size):
             r = r0 + i
-            down, p, up = ps[i:i + 3]
-            right, left = sides[i + 1]
-            dx, dy = dxs[i + 1], up - down
+            p, up, down = kry[n, r], kry[n, r + 1], kry[n, r - 1]
+            if i > 0:
+                below_dx, here, above = here[2], above, sides(r + 1)
+            right, left, dx = here
+            dy = up - down
             out.append(
                 coef[r, 0] * right + coef[r, 1] * left + coef[r, 2] * up + coef[r, 3] * down
                 + coef[r, 4] * zp(p) + coef[r, 5] * zm(p) + coef[r, 6] * p
-                + coef[r, 7] * (dxs[i + 2] - dxs[i])
+                + coef[r, 7] * (above[2] - below_dx)
                 + coef[r, 8] * (zp(dx) - zm(dx)) + coef[r, 9] * (zp(dy) - zm(dy)))
         return out
 
@@ -388,31 +407,17 @@
     tile = jnp.zeros((16, 128), jnp.float32)
     for n, s in enumerate(sums):
         tile = jnp.where(spot == n, jnp.sum(s, axis=0, keepdims=True), tile)
-    part[...] = tile
-
-    def x_copy(d):
-        k = 28 + d - 1
+    half = lane < 64
+    folded = tile + pltpu.roll(tile, 64, 1)
+    part[...] = jnp.where(half[:8], folded[:8], folded[8:])
+
+    def part_copy(d):
         return pltpu.make_async_remote_copy(
-            src_ref=part, dst_ref=part_x.at[d - 1], send_sem=send_sem.at[k], recv_sem=recv_sem.at[k],
-            device_id={"gx": lax.rem(gx + d, nx), "gy": gy}, device_id_type=MESH)
-
-    def y_copy(d):
-        k = 28 + nx - 1 + d - 1
-        return pltpu.make_async_remote_copy(
-            src_ref=sum_x, dst_ref=part_y.at[d - 1], send_sem=send_sem.at[k], recv_sem=recv_sem.at[k],
-            device_id={"gx": gx, "gy": lax.rem(gy + d, ny)}, device_id_type=MESH)
-
-    for d in range(1, nx):
-        x_copy(d).start()
+            src_ref=part, dst_ref=parts.at[d - 1], send_sem=send_sem.at[27 + d],
+            recv_sem=recv_sem.at[27 + d], device_id=peer(d), device_id_type=MESH)
+
+    every_peer(lambda d: part_copy(d).start())
     upwind(((3, TH),), 2, 12, 5)
-    for d in range(1, nx):
-        x_copy(d).wait_recv()
-    tile = part[...]
-    for d in range(1, nx):
-        tile = tile + part_x[d - 1]
-    sum_x[...] = tile
-    for d in range(1, ny):
-        y_copy(d).start()
     antidiffuse((3,), 3, 11, 4)
 
     def store(ref, base, j, value):
@@ -420,15 +425,18 @@
 
     for j in range(ny_dev):
         store(th_out, 0, j, second[3 + j, 3][:, :128])
-    for d in range(1, ny):
-        y_copy(d).wait_recv()
-    tile = sum_x[...]
-    for d in range(1, ny):
-        tile = tile + part_y[d - 1]
-    total = jnp.sum(tile, axis=1, keepdims=True)
+    every_peer(lambda d: part_copy(d).wait_recv())
+    if count <= 64:
+        tile = part[...]
+        for d in range(1, count):
+            tile = tile + parts[d - 1]
+    else:
+        tile = lax.fori_loop(1, count, lambda d, acc: acc + parts[d - 1], part[...])
+    low = jnp.sum(jnp.where(half[:8], tile, 0.0), axis=1, keepdims=True)
+    high = jnp.sum(jnp.where(half[:8], 0.0, tile), axis=1, keepdims=True)
     gmat = {}
     for n, (a, b) in enumerate(pairs):
-        gmat[a, b] = gmat[b, a] = total[n:n + 1, :]
+        gmat[a, b] = gmat[b, a] = low[n:n + 1, :] if n < 8 else high[n - 8:n - 7, :]
 
     def dot(a, b):
         terms = [x * y for x, y in zip(a, b) if x is not None and y is not None]
@@ -493,10 +501,7 @@
     wait_send(half_a)
     wait_send(half_b)
     wait_send(half_r)
-    for d in range(1, nx):
-        x_copy(d).wait_send()
-    for d in range(1, ny):
-        y_copy(d).wait_send()
+    every_peer(lambda d: part_copy(d).wait_send())
 
 
 def solution(mesh):
@@ -505,11 +510,11 @@
     def local(momenta, theta, courant, density, metric_diag, metric_cross):
         nz, ny_dev, nx_dev = density.shape
         args = (momenta, theta, courant, density, metric_diag, metric_cross)
-        flat = [a.reshape(-1, nx_dev) for a in args]
+        flat = [pltpu.with_memory_space_constraint(a.reshape(-1, nx_dev), pltpu.HBM) for a in args]
         plane = nz * ny_dev
         f32 = jnp.float32
         n_ext = ny_dev + 6
-        n_sem = 28 + nx - 1 + ny - 1
+        n_sem = 28 + nx * ny - 1
         shape = jax.ShapeDtypeStruct
         vmem = pltpu.VMEM
         mom, th, press = pl.pallas_call(
@@ -533,16 +538,14 @@
                 vmem((nz, nx_dev), f32),
                 vmem((2, nz, nx_dev), f32),
                 vmem((2, 2, nz, nx_dev), f32),
-                vmem((16, 128), f32),
-                vmem((nx - 1, 16, 128), f32),
-                vmem((16, 128), f32),
-                vmem((ny - 1, 16, 128), f32),
+                vmem((8, 128), f32),
+                vmem((nx * ny - 1, 8, 128), f32),
                 pltpu.SemaphoreType.DMA((6,)),
                 pltpu.SemaphoreType.DMA((n_sem,)),
                 pltpu.SemaphoreType.DMA((n_sem,)),
             ],
             compiler_params=pltpu.CompilerParams(
-                collective_id=0, has_side_effects=True, vmem_limit_bytes=60 * 1024 * 1024),
+                collective_id=0, has_side_effects=True, vmem_limit_bytes=40 * 1024 * 1024),
         )(*flat)
         return mom.reshape(momenta.shape), th.reshape(theta.shape), press.reshape(theta.shape)
 

time: 29.8 us -> 27.8 us (0.933)
  local copies, waits for them, and re-layouts: 3.14 us -> 1.94 us
  Pallas kernels: 25.8 us -> 25.1 us
    unnamed x7 -> x3, local copies, waits for them, and re-layouts: 3.14 us -> 1.94 us
    pallas_call x1, Pallas kernels: 25.8 us -> 25.1 us  [local(): pl.pallas_call(functools.partial(kernel, nx, ny), out_shape=(shape((3 * p...]
where the time goes in v5:
time: 27.8 us; the launch traced here: 27.7 us
  Pallas kernels  25.1 us (90%)
  local copies, waits for them, and re-layouts  1.94 us (7%)
  between operations  0.64 us (2%)
    pallas_call x1, Pallas kernels, local(): pl.pallas_call(functools.partial(kernel, nx, ny), out_shape=(shape((3 * p...  25.1 us
    unnamed x3, local copies, waits for them, and re-layouts  1.94 us

profile of v5, /device:TPU:0, one launch (start us, length us, event | category | flops | bytes accessed | tf_op | source)
XLA Modules:
  0.0 27.7 jit_solution(2850327975569682728)
XLA Ops:
  0.6 25.1 %shard_map.85 = (f32[384,128]{1,0:T(8,128)S(1)}, f32[128,128]{1,0:T(8,128)S(1)}, f32[128,128]{1,0:T(8,128)S(1)}) custom-call(f32[384,128]{1,0:T(8,128)} %bitcast.12, f32[128,128]{1,0:T(8,128)} %bitcast.16, f32[384,128]{1,0:T(8,128)} %bitcast.13, f32[128,128]{1,0:T(8,128)} %bitcast.17, f32[384,128]{1,0:T(8,128)} %bitcast.14, f32[384,128]{1,0:T(8,128)} %bitcast.15), custom_call_target="tpu_custom_call" | custom-call | tf_op jit(solution)/shard_map/pallas_call | solution.py:520
  25.8 0.7 %copy.12 = f32[3,16,8,128]{3,2,1,0:T(8,128)} copy(f32[3,16,8,128]{3,2,1,0:T(8,128)S(1)} %bitcast.9) | data formatting | bytes 393216
  26.4 0.6 %copy.13 = f32[16,8,128]{2,1,0:T(8,128)} copy(f32[16,8,128]{2,1,0:T(8,128)S(1)} %bitcast.11) | data formatting | bytes 131072
  27.1 0.6 %copy.14 = f32[16,8,128]{2,1,0:T(8,128)} copy(f32[16,8,128]{2,1,0:T(8,128)S(1)} %bitcast.10) | data formatting | bytes 131072

commit v6 on v5

--- a/solution.py
+++ b/solution.py
@@ -93,15 +93,8 @@
 
     def grouped(lo, hi, size, body, stride=None):
         stride = size if stride is None else stride
-        count = (hi - lo) // stride
-        if count == 1:
-            body(lo)
-            return
-
-        def step(n, _):
-            body(lo + n * stride)
-            return 0
-        lax.fori_loop(0, count, step, 0)
+        for r0 in range(lo, lo + (hi - lo) // stride * stride, stride):
+            body(r0)
 
     def load_half(b):
         def some(j0):
@@ -116,7 +109,7 @@
         grouped(0, ny_dev, 2, some)
 
     def pack_half(b):
-        def one(t, _):
+        for t in range(ny_dev // 2):
             acc = jnp.zeros((nz, 128), jnp.float32)
             for side in range(2):
                 for fi in range(HALF):
@@ -128,8 +121,6 @@
                 moved = pltpu.roll(rows[5 + 3 * (t // 2), b * HALF + fi], (p + 4) % 128, 1)
                 acc = jnp.where(slot == p // 8, moved, acc)
             packed[b, t] = acc
-            return 0
-        lax.fori_loop(0, ny_dev // 2, one, 0)
 
     def spread(b, tile, side, row):
         for fi in range(HALF):
@@ -137,12 +128,10 @@
             edges[row, b * HALF + fi] = pltpu.roll(tile, (128 - (p + 4)) % 128, 1)
 
     def unpack_own(b):
-        def one(t, _):
+        for t in range(ny_dev // 2):
             tile = jnp.where(from_left, beside[b, 0, t], beside[b, 1, t])
             for side in range(2):
                 spread(b, tile, side, 3 + 2 * t + side)
-            return 0
-        lax.fori_loop(0, ny_dev // 2, one, 0)
 
     def unpack_halo(b):
         def one(side, near, third):
@@ -222,9 +211,12 @@
     for n in (0, 2, 3):
         loads[n].wait()
     load_half(0)
+    pl.semaphore_wait(barrier, count - 1)
+    straight = {1: half_a[1][:2], -1: half_a[-1][:2], 0: []}
+    strips = {1: half_a[1][2:], -1: half_a[-1][2:], 0: half_a[0]}
+    start(straight)
     pack_half(0)
-    pl.semaphore_wait(barrier, count - 1)
-    start(half_a)
+    start(strips)
     for n in (1, 4, 5):
         loads[n].wait()
     load_half(1)
@@ -402,7 +394,7 @@
     halo_rhs(1, (0, 1, 2), 11, gy < ny - 1)
     lift(0, 1, 19, 3, 9)
     lift(1, 2, 16, 3, 7)
-    sums = lax.fori_loop(0, 2, lambda n, acc: gram(acc, 3 + 5 * n, 3), sums)
+    sums = gram(gram(sums, 3, 3), 8, 3)
     spot = lax.broadcasted_iota(jnp.int32, (16, 128), 0)
     tile = jnp.zeros((16, 128), jnp.float32)
     for n, s in enumerate(sums):

time: 27.8 us -> 27.7 us (level)
  no operation moved by 1% of the time
where the time goes in v6:
time: 27.7 us; the launch traced here: 27.6 us
  Pallas kernels  25 us (90%)
  local copies, waits for them, and re-layouts  1.94 us (7%)
  between operations  0.64 us (2%)
    pallas_call x1, Pallas kernels, local(): pl.pallas_call(functools.partial(kernel, nx, ny), out_shape=(shape((3 * p...  25 us
    unnamed x3, local copies, waits for them, and re-layouts  1.94 us

profile of v6, /device:TPU:0, one launch (start us, length us, event | category | flops | bytes accessed | tf_op | source)
XLA Modules:
  0.0 27.6 jit_solution(5659972815505464761)
XLA Ops:
  0.6 25.0 %shard_map.85 = (f32[384,128]{1,0:T(8,128)S(1)}, f32[128,128]{1,0:T(8,128)S(1)}, f32[128,128]{1,0:T(8,128)S(1)}) custom-call(f32[384,128]{1,0:T(8,128)} %bitcast.12, f32[128,128]{1,0:T(8,128)} %bitcast.16, f32[384,128]{1,0:T(8,128)} %bitcast.13, f32[128,128]{1,0:T(8,128)} %bitcast.17, f32[384,128]{1,0:T(8,128)} %bitcast.14, f32[384,128]{1,0:T(8,128)} %bitcast.15), custom_call_target="tpu_custom_call" | custom-call | tf_op jit(solution)/shard_map/pallas_call | solution.py:512
  25.6 0.7 %copy.12 = f32[3,16,8,128]{3,2,1,0:T(8,128)} copy(f32[3,16,8,128]{3,2,1,0:T(8,128)S(1)} %bitcast.9) | data formatting | bytes 393216
  26.3 0.6 %copy.13 = f32[16,8,128]{2,1,0:T(8,128)} copy(f32[16,8,128]{2,1,0:T(8,128)S(1)} %bitcast.11) | data formatting | bytes 131072
  26.9 0.6 %copy.14 = f32[16,8,128]{2,1,0:T(8,128)} copy(f32[16,8,128]{2,1,0:T(8,128)S(1)} %bitcast.10) | data formatting | bytes 131072

commit v7 on v6

--- a/solution.py
+++ b/solution.py
@@ -180,7 +180,7 @@
         each(by, lambda c: c.wait_send(), 1)
 
     def half_entries(b):
-        fs = pl.ds(b * HALF, HALF)
+        fs = pl.ds(b * HALF, HALF - b)
         ft = pl.ds(b * HALF, THIRD[b])
         return [
             (0, 1, rows.at[pl.ds(9, 2), fs], rows.at[pl.ds(1, 2), fs]),
@@ -197,6 +197,11 @@
 
     half_a = group(half_entries(0), 0)
     half_b = group(half_entries(1), 10)
+    theta = pl.ds(TH, 1)
+    half_t = group([
+        (0, 1, rows.at[pl.ds(9, 2), theta], rows.at[pl.ds(1, 2), theta]),
+        (0, -1, rows.at[pl.ds(3, 2), theta], rows.at[pl.ds(11, 2), theta]),
+    ], 27 + count)
     half_r = group([
         (0, 1, rhs_rows.at[pl.ds(8, 3)], rhs_rows.at[pl.ds(0, 3)]),
         (0, -1, rhs_rows.at[pl.ds(3, 3)], rhs_rows.at[pl.ds(11, 3)]),
@@ -291,6 +296,7 @@
         acc = jnp.where(slot == j, pltpu.roll(value, 8 * j + 4, 1), acc)
     rhs_packed[...] = acc
     start(half_r)
+    start(half_t)
 
     wait_beside(half_b)
     unpack_own(1)
@@ -409,6 +415,7 @@
             recv_sem=recv_sem.at[27 + d], device_id=peer(d), device_id_type=MESH)
 
     every_peer(lambda d: part_copy(d).start())
+    wait_halo(half_t)
     upwind(((3, TH),), 2, 12, 5)
     antidiffuse((3,), 3, 11, 4)
 
@@ -493,6 +500,7 @@
     wait_send(half_a)
     wait_send(half_b)
     wait_send(half_r)
+    wait_send(half_t)
     every_peer(lambda d: part_copy(d).wait_send())
 
 
@@ -506,7 +514,7 @@
         plane = nz * ny_dev
         f32 = jnp.float32
         n_ext = ny_dev + 6
-        n_sem = 28 + nx * ny - 1
+        n_sem = 28 + nx * ny - 1 + 2
         shape = jax.ShapeDtypeStruct
         vmem = pltpu.VMEM
         mom, th, press = pl.pallas_call(

time: 27.7 us -> 27.9 us (level)
  no operation moved by 1% of the time
where the time goes in v7:
time: 27.9 us; the launch traced here: 27.8 us
  Pallas kernels  25.2 us (90%)
  local copies, waits for them, and re-layouts  1.94 us (7%)
  between operations  0.64 us (2%)
    pallas_call x1, Pallas kernels, local(): pl.pallas_call(functools.partial(kernel, nx, ny), out_shape=(shape((3 * p...  25.2 us
    unnamed x3, local copies, waits for them, and re-layouts  1.94 us

profile of v7, /device:TPU:0, one launch (start us, length us, event | category | flops | bytes accessed | tf_op | source)
XLA Modules:
  0.0 27.8 jit_solution(14488352476401059733)
XLA Ops:
  0.6 25.2 %shard_map.85 = (f32[384,128]{1,0:T(8,128)S(1)}, f32[128,128]{1,0:T(8,128)S(1)}, f32[128,128]{1,0:T(8,128)S(1)}) custom-call(f32[384,128]{1,0:T(8,128)} %bitcast.12, f32[128,128]{1,0:T(8,128)} %bitcast.16, f32[384,128]{1,0:T(8,128)} %bitcast.13, f32[128,128]{1,0:T(8,128)} %bitcast.17, f32[384,128]{1,0:T(8,128)} %bitcast.14, f32[384,128]{1,0:T(8,128)} %bitcast.15), custom_call_target="tpu_custom_call" | custom-call | tf_op jit(solution)/shard_map/pallas_call | solution.py:520
  25.9 0.7 %copy.12 = f32[3,16,8,128]{3,2,1,0:T(8,128)} copy(f32[3,16,8,128]{3,2,1,0:T(8,128)S(1)} %bitcast.9) | data formatting | bytes 393216
  26.5 0.6 %copy.13 = f32[16,8,128]{2,1,0:T(8,128)} copy(f32[16,8,128]{2,1,0:T(8,128)S(1)} %bitcast.11) | data formatting | bytes 131072
  27.2 0.6 %copy.14 = f32[16,8,128]{2,1,0:T(8,128)} copy(f32[16,8,128]{2,1,0:T(8,128)S(1)} %bitcast.10) | data formatting | bytes 131072
